TPU v7x, 32 devices: a whole 2x2x4 slice. The times are simulated.
32 devices in a mesh: pix: 8 (over y, x, core), site: 4 (over z).
Axes of the slice: x: 2, y: 2, z: 4, core: 2. Of those that a mesh axis runs over, the one named last changes fastest.
Arguments:
- margins: int32 [128, 256, 512], P('pix', None, 'site'), may hold values from -2047 to 2047
- block_pos: int32 [128, 4], P('pix', 'site'), may hold values from -1 to 15, as said below
- pattern_ids: int32 [512], P('site'), may hold values from 0 to 15
- pattern_gain: float32 [16, 256], replicated, may hold values from -4 to 4
- site_price: float32 [512], P('site'), may hold values from 0.2 to 4
- weights: float32 [32768], P('pix'), may hold values from 0.2 to 2
- site_start: float32 [512], P('site'), may hold values from 0 to 1
- pixel_start: float32 [32768], P('pix'), may hold values from 0 to 1
- dual_start: float32 [32768], P('pix'), may hold values from 0 to 2
Outputs:
- site_level: float32 [512], P('site')
- pixel_level: float32 [32768], P('pix')
- duals: float32 [32768], P('pix')
Inputs may be any that keep to these rules, and one draw needn't show every extreme that they name: Row k of block_pos and of margins is held by pixel device k // 16 and belongs to pixel device (k // 2) % 8; its entry for site block b is the position, among that device's 16 pixel blocks, of the pixel block of the tile, or -1 for an empty slot. The lists are filled unevenly. For one pixel device, drawn afresh, every slot that belongs to it is filled in every row group and site block.
All inputs are finite; a program needn't handle non-finite values.
Results may differ from a plain program's by a relative error of at most 0.0003.
Values may be sent and summed in bfloat16 or wider, within the bound.
A program may use at most 64 MiB of HBM per device.

v0:
```python
import jax
import jax.numpy as jnp
from jax import lax
from jax.sharding import PartitionSpec as P

ITERS = 2


MARGIN_SCALE = 2.0 ** (-9)


def build_tiles(margins, block_pos, pattern_ids, pattern_gain):
    patterns = pattern_gain.shape[0]
    chooser = (pattern_ids[:, None] == jnp.arange(patterns, dtype=jnp.int32)[None, :]).astype(
        jnp.float32
    )
    gain_tile = lax.dot_general(
        pattern_gain, chooser, (((0,), (1,)), ((), ())), precision=lax.Precision.HIGHEST
    )
    filled = block_pos[:, 0] >= 0
    values = jax.nn.sigmoid(margins.astype(jnp.float32) * MARGIN_SCALE + gain_tile[None])
    return jnp.where(filled[:, None, None], values, 0.0).astype(jnp.bfloat16)


def local(
    margins,
    block_pos,
    pattern_ids,
    pattern_gain,
    site_price,
    weights,
    site_start,
    pixel_start,
    dual_start,
):
    slot_count = margins.shape[0]
    block_width = pattern_gain.shape[1]
    blocks = weights.shape[0] // block_width
    coverage = build_tiles(margins, block_pos, pattern_ids, pattern_gain)
    position = block_pos[:, 0]
    tiles_here, arrived = (
        lax.all_to_all(coverage, "pix", split_axis=0, concat_axis=0, tiled=True),
        lax.all_to_all(
            position.astype(jnp.bfloat16), "pix", split_axis=0, concat_axis=0, tiled=True
        ),
    )
    chooser = arrived.astype(jnp.float32)[:, None] == jnp.arange(blocks, dtype=jnp.float32)[None, :]
    chooser_half = chooser.astype(jnp.bfloat16)
    chooser_full = chooser.astype(jnp.float32)

    def spread_rows(products):
        return jnp.einsum("kb,tkr->btr", chooser_full, products, precision=lax.Precision.HIGHEST)

    def column_totals(selected):
        partial_value = jnp.einsum(
            "tkr,krj->tj", selected, tiles_here, preferred_element_type=jnp.float32
        )
        return lax.psum(partial_value, "pix")

    def row_totals(values):
        products = jnp.einsum("krj,tj->tkr", tiles_here, values, preferred_element_type=jnp.float32)
        return lax.psum(spread_rows(products), "site")

    ones_pixels = jnp.ones((1, slot_count, block_width), jnp.bfloat16)
    ones_sites = jnp.ones((1, tiles_here.shape[2]), jnp.bfloat16)
    site_level, pixel_level, duals = (site_start, pixel_start, dual_start)
    for iteration in range(ITERS):
        dual_half = duals.astype(jnp.bfloat16).reshape(blocks, block_width)
        selected = jnp.dot(chooser_half, dual_half, preferred_element_type=jnp.float32).astype(
            jnp.bfloat16
        )[None]
        if iteration == 0:
            totals = column_totals(jnp.concatenate([selected, ones_pixels], 0))
            pulled = totals[0]
            column_sum = totals[1]
        else:
            pulled = column_totals(selected)[0]
        new_site = jnp.clip(site_level - (site_price - pulled / column_sum), 0.0, 1.0)
        new_pixel = jnp.clip(pixel_level - (duals - weights), 0.0, 1.0)
        extrapolated = (2.0 * new_site - site_level).astype(jnp.bfloat16)[None]
        if iteration == 0:
            spread = row_totals(jnp.concatenate([extrapolated, ones_sites], 0))
            pushed = spread[:, 0, :].reshape(-1)
            row_sum = spread[:, 1, :].reshape(-1)
        else:
            pushed = row_totals(extrapolated)[:, 0, :].reshape(-1)
        duals = jnp.maximum(duals + (2.0 * new_pixel - pixel_level - pushed) / (row_sum + 1.0), 0.0)
        site_level, pixel_level = (new_site, new_pixel)
    return (site_level, pixel_level, duals)


def solution(mesh):
    placed = (
        P("pix", None, "site"),
        P("pix", "site"),
        P("site"),
        P(),
        P("site"),
        P("pix"),
        P("site"),
        P("pix"),
        P("pix"),
    )
    return jax.shard_map(
        local,
        mesh=mesh,
        in_specs=placed,
        out_specs=(P("site"), P("pix"), P("pix")),
        check_vma=False,
    )
```

profile of v0, /device:TPU:0, one launch (start us, length us, event | category | flops | bytes accessed | tf_op | source)
XLA Modules:
  0.0 92.8 jit_solution(18040317809073812055)
XLA Ops:
  0.6 0.0 copy-start
  0.6 0.7 convert_reduce_fusion.1
  1.3 0.7 convert_element_type.63
  2.0 5.2 %all-to-all-start = ((bf16[8,2,1]{1,2,0:T(2,128)(2,1)}), bf16[8,2,1]{1,2,0:T(2,128)(2,1)S(1)}, u32[]{:S(2)}, u32[]{:S(2)}) async-start(bf16[8,2,1]{1,2,0:T(2,128)(2,1)} %convert_element_type.63), calls=%async_computation | async-start | bytes 8192 | tf_op jit(solution)/shard_map/all_to_all | solution.py:43
  7.2 0.7 compare_bitcast_fusion
  7.8 0.0 copy-done
  7.8 0.9 convolution_bitcast_fusion
  8.8 0.1 copy.17
  8.9 0.0 copy-start.1
  8.9 3.2 %select_convert_fusion = bf16[16,256,128]{2,1,0:T(8,128)(2,1)} fusion(s32[16,256,128]{2,1,0:T(8,128)} %param.9, f32[256,128]{1,0:T(8,128)S(1)} %copy.17, pred[16]{0:T(512)(128)(4,1)S(1)} %compare_bitcast_fusion), kind=kLoop, calls=%fused_computation | loop fusion | flops 4194304 | bytes 3276816 | tf_op jit(solution)/shard_map/convert_element_type | solution.py:22
  12.1 0.0 copy-start.5
  12.1 0.0 copy-start.6
  12.1 0.0 copy-start.2
  12.1 0.0 copy-start.3
  12.1 0.0 all-to-all-done
  12.1 4.3 %all-to-all-start.1 = ((bf16[16,256,128]{2,1,0:T(8,128)(2,1)}), bf16[16,256,128]{2,1,0:T(8,128)(2,1)S(1)}, u32[]{:S(2)}, u32[]{:S(2)}) async-start(bf16[16,256,128]{2,1,0:T(8,128)(2,1)} %select_convert_fusion), calls=%async_computation.1 | async-start | bytes 2097152 | tf_op jit(solution)/shard_map/all_to_all | solution.py:42
  16.4 0.0 copy-done.1
  16.5 0.1 reshape.57
  16.6 0.2 fusion
  16.8 15.1 %all-to-all-done.1 = bf16[16,256,128]{2,1,0:T(8,128)(2,1)S(1)} async-done(((bf16[16,256,128]{2,1,0:T(8,128)(2,1)}), bf16[16,256,128]{2,1,0:T(8,128)(2,1)S(1)}, u32[]{:S(2)}, u32[]{:S(2)}) %all-to-all-start.1) | async-done | bytes 1048608 | tf_op jit(solution)/shard_map/all_to_all | solution.py:42
  31.9 0.3 convolution_bitcast_fusion.2
  32.1 11.8 %psum.28 = f32[2,128]{1,0:T(2,128)S(1)} all-reduce(f32[2,128]{1,0:T(2,128)S(1)} %convolution_bitcast_fusion.2), channel_id=1, replica_groups=mesh['pix'=8,'site'=4] {'pix'}, use_global_device_ids=true, to_apply=%region_0.1 | all-reduce | flops 256 | bytes 2048 | tf_op jit(solution)/shard_map/psum | solution.py:58
  43.9 0.0 copy-done.5
  43.9 0.0 copy-done.6
  43.9 0.4 fusion.20
  44.3 0.2 fusion.2
  44.5 19.3 %psum.29 = f32[16,2,256]{2,0,1:T(8,128)S(1)} all-reduce(f32[16,2,256]{2,0,1:T(8,128)S(1)} %fusion.2), channel_id=1, replica_groups=mesh['pix'=8,'site'=4] {'site'}, use_global_device_ids=true, to_apply=%region_1.2 | all-reduce | flops 8192 | bytes 65536 | tf_op jit(solution)/shard_map/psum | solution.py:62
  63.8 0.0 copy-done.2
  63.8 0.0 copy-done.3
  63.9 0.2 fusion.1
  64.1 0.2 convolution_bitcast_fusion.3
  64.3 11.8 %psum.30 = f32[1,128]{1,0:T(1,128)S(1)} all-reduce(f32[1,128]{1,0:T(1,128)S(1)} %convolution_bitcast_fusion.3), channel_id=1, replica_groups=mesh['pix'=8,'site'=4] {'pix'}, use_global_device_ids=true, to_apply=%region_2.3 | all-reduce | flops 128 | bytes 1024 | tf_op jit(solution)/shard_map/psum | solution.py:58
  76.1 0.0 copy-start.4
  76.1 0.4 fusion.16
  76.5 0.1 convolution_bitcast_fusion.1
  76.7 15.5 %psum.31 = f32[4096]{0:T(1024)S(1)} all-reduce(f32[4096]{0:T(1024)S(1)} %bitcast.63), channel_id=1, replica_groups=mesh['pix'=8,'site'=4] {'site'}, use_global_device_ids=true, to_apply=%region_3.4 | all-reduce | flops 4096 | bytes 32768 | tf_op jit(solution)/shard_map/psum | solution.py:62
  92.2 0.6 add_maximum_fusion
  92.8 0.0 copy-done.4
  (12 shorter events, 0.1 us)
Async XLA Ops:
  0.6 7.2 %copy-start = (f32[16,256]{1,0:T(8,128)S(1)}, f32[16,256]{1,0:T(8,128)}, u32[]{:S(2)}) copy-start(f32[16,256]{1,0:T(8,128)} %param.12) | copy-start | bytes 49156
  2.0 10.1 %all-to-all-start = ((bf16[8,2,1]{1,2,0:T(2,128)(2,1)}), bf16[8,2,1]{1,2,0:T(2,128)(2,1)S(1)}, u32[]{:S(2)}, u32[]{:S(2)}) async-start(bf16[8,2,1]{1,2,0:T(2,128)(2,1)} %convert_element_type.63), calls=%async_computation | async-start | bytes 8192 | tf_op jit(solution)/shard_map/all_to_all | solution.py:43
  8.9 7.6 %copy-start.1 = (f32[4096]{0:T(1024)S(1)}, f32[4096]{0:T(1024)}, u32[]{:S(2)}) copy-start(f32[4096]{0:T(1024)} %param.17) | copy-start | bytes 49156
  12.1 31.8 %copy-start.5 = (f32[128]{0:T(128)S(1)}, f32[128]{0:T(128)}, u32[]{:S(2)}) copy-start(f32[128]{0:T(128)} %param.13) | copy-start | bytes 1540
  12.1 31.8 %copy-start.6 = (f32[128]{0:T(128)S(1)}, f32[128]{0:T(128)}, u32[]{:S(2)}) copy-start(f32[128]{0:T(128)} %param.15) | copy-start | bytes 1540
  12.1 51.7 %copy-start.2 = (f32[4096]{0:T(1024)S(1)}, f32[4096]{0:T(1024)}, u32[]{:S(2)}) copy-start(f32[4096]{0:T(1024)} %param.16) | copy-start | bytes 49156
  12.1 51.7 %copy-start.3 = (f32[4096]{0:T(1024)S(1)}, f32[4096]{0:T(1024)}, u32[]{:S(2)}) copy-start(f32[4096]{0:T(1024)} %param.14) | copy-start | bytes 49156
  12.1 19.8 %all-to-all-start.1 = ((bf16[16,256,128]{2,1,0:T(8,128)(2,1)}), bf16[16,256,128]{2,1,0:T(8,128)(2,1)S(1)}, u32[]{:S(2)}, u32[]{:S(2)}) async-start(bf16[16,256,128]{2,1,0:T(8,128)(2,1)} %select_convert_fusion), calls=%async_computation.1 | async-start | bytes 2097152 | tf_op jit(solution)/shard_map/all_to_all | solution.py:42
  76.1 16.7 %copy-start.4 = (f32[128]{0:T(128)}, f32[128]{0:T(128)S(1)}, u32[]{:S(2)}) copy-start(f32[128]{0:T(128)S(1)} %fusion.19) | copy-start | bytes 1540
where the time goes:
time: 93.3 us; the launch traced here: 92.8 us
  blocking collectives  58.4 us (63%)
  waiting for transfers between devices  15.1 us (16%)
  starting transfers between devices  9.51 us (10%)
  other arithmetic  5.25 us (6%)
  matrix products  2.83 us (3%)
  local copies, waits for them, and re-layouts  0.96 us (1%)
    psum x2, blocking collectives, row_totals(): return lax.psum(spread_rows(products), 'site')  34.8 us
    psum x2, blocking collectives, column_totals(): return lax.psum(partial_value, 'pix')  23.6 us
    all_to_all x1, waiting for transfers between devices, local(): lax.all_to_all(coverage, 'pix', split_axis=0, concat_axis=0, tiled=True)  15.1 us
    all_to_all x1, starting transfers between devices, local(): lax.all_to_all(position.astype(jnp.bfloat16), 'pix', split_axis=0, concat...  5.17 us
    all_to_all x1, starting transfers between devices, local(): lax.all_to_all(coverage, 'pix', split_axis=0, concat_axis=0, tiled=True)  4.34 us
    convert_element_type x1, other arithmetic, build_tiles(): return jnp.where(filled[:, None, None], values, 0.0).astype(jnp.bfloat16)  3.22 us
  transfers between devices with their start and end apart: 2, of which 1 were waited for; matrix products, arithmetic and copies ran while one was open for 6% of the time, Pallas kernels for 0%

commit v1 on v0

v1 whole, which is shorter than its diff:
```python
import functools

import jax
import jax.numpy as jnp
from jax import lax
from jax.experimental import pallas as pl
from jax.experimental.pallas import tpu as pltpu
from jax.sharding import PartitionSpec as P

ITERS = 2
MARGIN_SCALE = 2.0 ** (-9)
LANES = 128
MESH = pl.DeviceIdType.MESH
NT = (((1,), (1,)), ((), ()))


def kernel(
    npix,
    nsite,
    margins_ref,
    pos_ref,
    ids_ref,
    gain_ref,
    price_ref,
    weights_ref,
    site_ref,
    pixel_ref,
    dual_ref,
    site_out,
    pixel_out,
    dual_out,
    margins_v,
    tiles,
    dual_all,
    row_send,
    row_recv,
    col_recv,
    push_send,
    push_recv,
    level_recv,
    margin_sem,
    dual_sem,
    row_sem,
    col_sem,
    push_sem,
    level_sem,
):
    slots, width, sites = margins_v.shape
    cap = slots // npix
    halves = width // LANES
    rows = dual_ref.shape[0]
    me = lax.axis_index("pix")
    here = lax.axis_index("site")

    def pix_peer(step):
        return lax.rem(me + step, npix)

    def site_peer(step):
        return lax.rem(here + step, nsite)

    def margin_copy(t):
        part = pl.ds(t * cap, cap)
        return pltpu.make_async_copy(margins_ref.at[part], margins_v.at[part], margin_sem.at[t])

    for t in range(npix):
        margin_copy(t).start()

    barrier = pltpu.get_barrier_semaphore()
    for step in range(1, npix):
        pl.semaphore_signal(barrier, inc=1, device_id=(pix_peer(step), here), device_id_type=MESH)
    for step in range(1, nsite):
        pl.semaphore_signal(barrier, inc=1, device_id=(me, site_peer(step)), device_id_type=MESH)

    def send_pix(src, dst, sems, step):
        pltpu.make_async_remote_copy(
            src_ref=src,
            dst_ref=dst,
            send_sem=sems.at[0],
            recv_sem=sems.at[1],
            device_id=(pix_peer(step), here),
            device_id_type=MESH,
        ).start()

    def send_site(src, dst, sems, step):
        pltpu.make_async_remote_copy(
            src_ref=src,
            dst_ref=dst,
            send_sem=sems.at[0],
            recv_sem=sems.at[1],
            device_id=(me, site_peer(step)),
            device_id_type=MESH,
        ).start()

    def drain(buffer, sem):
        part = buffer.at[pl.ds(0, buffer.shape[0] - 1)]
        pltpu.make_async_copy(part, part, sem).wait()

    def share_duals(i, values):
        dual_all[i, pl.ds(me, 1)] = values.astype(jnp.bfloat16)[None]

        def go():
            for step in range(1, npix):
                send_pix(dual_all.at[i, me], dual_all.at[i, me], dual_sem.at[i], step)

        return go

    go = share_duals(0, dual_ref[...])
    pl.semaphore_wait(barrier, npix + nsite - 2)
    go()

    pos = pos_ref[...]
    slot_col = lax.broadcasted_iota(jnp.int32, (slots, 1), 0)
    base = jnp.where(pos >= 0, (slot_col // cap) * rows + pos * halves, -halves)
    row_id = lax.broadcasted_iota(jnp.int32, (slots, npix * rows), 1)
    choosers = [
        (row_id == base + h).astype(jnp.float32).astype(jnp.bfloat16) for h in range(halves)
    ]
    pos_rows = jnp.broadcast_to(pos.astype(jnp.float32), (slots, LANES))
    for t in range(npix):
        row_send[t, halves * cap :, :] = pos_rows[t * cap : (t + 1) * cap]
    filled = jnp.broadcast_to((pos >= 0).astype(jnp.float32), (slots, width))
    slot_row = lax.broadcasted_iota(jnp.int32, (slots, width), 0)
    slot_lane = lax.broadcasted_iota(jnp.int32, (slots, LANES), 0)

    def of_target(t, values):
        return jnp.where(slot_row // cap == t, values, 0.0).astype(jnp.bfloat16)

    def column_fold(sums):
        total = jnp.zeros((1, LANES), jnp.float32)
        for c in range(cap):
            part = sums[:, c * LANES : (c + 1) * LANES]
            total = total + jnp.sum(
                jnp.where(slot_lane % cap == c, part, 0.0), axis=0, keepdims=True
            )
        return total

    lane_row = lax.broadcasted_iota(jnp.int32, (16, cap * LANES), 0)
    lane_cap = lax.broadcasted_iota(jnp.int32, (16, cap * LANES), 1) // LANES

    def spread_sites(values):
        wide = jnp.concatenate([values] * cap, axis=1)
        return jnp.where(lane_row == lane_cap, wide, 0.0).astype(jnp.bfloat16)

    chooser = (
        lax.broadcasted_iota(jnp.int32, (gain_ref.shape[0], sites), 0) == ids_ref[...]
    ).astype(jnp.float32)
    gain_half = 0.5 * lax.dot_general(
        gain_ref[...],
        chooser,
        (((0,), (0,)), ((), ())),
        precision=lax.Precision.HIGHEST,
        preferred_element_type=jnp.float32,
    )
    ones_sites = spread_sites(jnp.ones((1, LANES), jnp.float32))

    def put_rows(buffer, t, products):
        for h in range(halves):
            buffer[t, h * cap : (h + 1) * cap, :] = products[:cap, h * LANES : (h + 1) * LANES]

    def build(t, sums):
        margin_copy(t).wait()
        for c in range(cap):
            values = margins_v[t * cap + c].astype(jnp.float32)
            values = 0.5 * jnp.tanh(values * (0.5 * MARGIN_SCALE) + gain_half) + 0.5
            tiles[t, :, c * LANES : (c + 1) * LANES] = values.astype(jnp.bfloat16)
        tile = tiles[t]
        put_rows(
            row_send,
            t,
            lax.dot_general(ones_sites, tile, NT, preferred_element_type=jnp.float32),
        )
        return sums + jnp.dot(of_target(t, filled), tile, preferred_element_type=jnp.float32)

    column_sums = lax.fori_loop(
        0, npix, build, jnp.zeros((slots, cap * LANES), jnp.float32)
    )
    col_recv[0, pl.ds(me, 1), 1:2] = column_fold(column_sums)[None]

    for step in range(1, npix):
        send_pix(row_send.at[pix_peer(step)], row_recv.at[me], row_sem, step)
    row_recv[pl.ds(me, 1)] = row_send[pl.ds(me, 1)]

    state_row = lax.broadcasted_iota(jnp.int32, (rows, LANES), 0).astype(jnp.float32)

    def gather_rows(buffer):
        total = jnp.zeros((rows, LANES), jnp.float32)
        for s in range(npix):
            for c in range(cap):
                at = row_recv[s, halves * cap + c : halves * cap + c + 1, :] * halves
                for h in range(halves):
                    line = buffer[s, h * cap + c : h * cap + c + 1, :]
                    total = total + jnp.where(state_row == at + h, line, 0.0)
        return total

    def share_levels(i, values):
        level_recv[i, pl.ds(here, 1)] = values[None]
        for step in range(1, nsite):
            send_site(level_recv.at[i, here], level_recv.at[i, here], level_sem.at[i], step)

    def total_levels(i):
        drain(level_recv.at[i], level_sem.at[i, 1])
        total = level_recv[i, 0]
        for z in range(1, nsite):
            total = total + level_recv[i, z]
        return total

    site_level = site_ref[...]
    pixel_level = pixel_ref[...]
    duals = dual_ref[...]
    column_sum = None
    row_sum = None
    for i in range(ITERS):
        drain(dual_all.at[i], dual_sem.at[i, 1])
        all_rows = dual_all[i].reshape(npix * rows, LANES)
        selected = jnp.concatenate(
            [jnp.dot(ch, all_rows, preferred_element_type=jnp.float32) for ch in choosers], axis=1
        )
        sums = jnp.zeros((slots, cap * LANES), jnp.float32)
        for t in range(npix):
            sums = sums + jnp.dot(
                of_target(t, selected), tiles[t], preferred_element_type=jnp.float32
            )
        col_recv[i, pl.ds(me, 1), 0:1] = column_fold(sums)[None]
        for step in range(1, npix):
            send_pix(col_recv.at[i, me], col_recv.at[i, me], col_sem.at[i], step)

        new_pixel = jnp.clip(pixel_level - (duals - weights_ref[...]), 0.0, 1.0)
        ahead = 2.0 * new_pixel - pixel_level
        if i == 0:
            drain(row_recv, row_sem.at[1])
            share_levels(ITERS, gather_rows(row_recv))

        drain(col_recv.at[i], col_sem.at[i, 1])
        pulled = col_recv[i, 0]
        for s in range(1, npix):
            pulled = pulled + col_recv[i, s]
        if i == 0:
            column_sum = pulled[1:2]
        new_site = jnp.clip(site_level - (price_ref[...] - pulled[0:1] / column_sum), 0.0, 1.0)
        ahead_sites = spread_sites(2.0 * new_site - site_level)
        for step in list(range(1, npix)) + [0]:
            t = pix_peer(step)
            put_rows(
                push_send.at[i],
                t,
                lax.dot_general(ahead_sites, tiles[t], NT, preferred_element_type=jnp.float32),
            )
            if step:
                send_pix(push_send.at[i, t], push_recv.at[i, me], push_sem.at[i], step)
        push_recv[i, pl.ds(me, 1)] = push_send[i, pl.ds(me, 1)]
        drain(push_recv.at[i], push_sem.at[i, 1])
        share_levels(i, gather_rows(push_recv.at[i]))
        if i == 0:
            row_sum = total_levels(ITERS)
        pushed = total_levels(i)
        duals = jnp.maximum(duals + (ahead - pushed) / (row_sum + 1.0), 0.0)
        if i < ITERS - 1:
            share_duals(i + 1, duals)()
        site_level, pixel_level = new_site, new_pixel

    site_out[...] = site_level
    pixel_out[...] = pixel_level
    dual_out[...] = duals

    drain(row_recv, row_sem.at[0])
    drain(level_recv.at[ITERS], level_sem.at[ITERS, 0])
    for i in range(ITERS):
        drain(dual_all.at[i], dual_sem.at[i, 0])
        drain(col_recv.at[i], col_sem.at[i, 0])
        drain(push_recv.at[i], push_sem.at[i, 0])
        drain(level_recv.at[i], level_sem.at[i, 0])


def local(
    npix,
    nsite,
    margins,
    block_pos,
    pattern_ids,
    pattern_gain,
    site_price,
    weights,
    site_start,
    pixel_start,
    dual_start,
):
    slots, width, sites = margins.shape
    cap = slots // npix
    halves = width // LANES
    rows = weights.shape[0] // LANES
    f32 = jnp.float32
    whole = pl.BlockSpec(memory_space=pltpu.VMEM)
    dma = pltpu.SemaphoreType.DMA
    site_level, pixel_level, duals = pl.pallas_call(
        functools.partial(kernel, npix, nsite),
        out_shape=(
            jax.ShapeDtypeStruct((1, sites), f32),
            jax.ShapeDtypeStruct((rows, LANES), f32),
            jax.ShapeDtypeStruct((rows, LANES), f32),
        ),
        in_specs=[pl.BlockSpec(memory_space=pl.ANY)] + [whole] * 8,
        out_specs=(whole, whole, whole),
        scratch_shapes=[
            pltpu.VMEM((slots, width, sites), jnp.int32),
            pltpu.VMEM((npix, width, cap * sites), jnp.bfloat16),
            pltpu.VMEM((ITERS, npix, rows, LANES), jnp.bfloat16),
            pltpu.VMEM((npix, (halves + 1) * cap, LANES), f32),
            pltpu.VMEM((npix, (halves + 1) * cap, LANES), f32),
            pltpu.VMEM((ITERS, npix, 2, LANES), f32),
            pltpu.VMEM((ITERS, npix, halves * cap, LANES), f32),
            pltpu.VMEM((ITERS, npix, halves * cap, LANES), f32),
            pltpu.VMEM((ITERS + 1, nsite, rows, LANES), f32),
            dma((npix,)),
            dma((ITERS, 2)),
            dma((2,)),
            dma((ITERS, 2)),
            dma((ITERS, 2)),
            dma((ITERS + 1, 2)),
        ],
        compiler_params=pltpu.CompilerParams(
            collective_id=0, has_side_effects=True, vmem_limit_bytes=40 * 1024 * 1024
        ),
    )(
        margins,
        block_pos,
        pattern_ids.reshape(1, sites),
        pattern_gain,
        site_price.reshape(1, sites),
        weights.reshape(rows, LANES),
        site_start.reshape(1, sites),
        pixel_start.reshape(rows, LANES),
        dual_start.reshape(rows, LANES),
    )
    return site_level.reshape(-1), pixel_level.reshape(-1), duals.reshape(-1)


def solution(mesh):
    placed = (
        P("pix", None, "site"),
        P("pix", "site"),
        P("site"),
        P(),
        P("site"),
        P("pix"),
        P("site"),
        P("pix"),
        P("pix"),
    )
    return jax.shard_map(
        functools.partial(local, mesh.shape["pix"], mesh.shape["site"]),
        mesh=mesh,
        in_specs=placed,
        out_specs=(P("site"), P("pix"), P("pix")),
        check_vma=False,
    )
```

time: 93.3 us -> 45.1 us (0.48)
  blocking collectives: 58.4 us -> 0 us
  Pallas kernels: 0 us -> 35 us
  waiting for transfers between devices: 15.1 us -> 0 us
  starting transfers between devices: 9.51 us -> 0 us
  local copies, waits for them, and re-layouts: 0.96 us -> 8.88 us
  other arithmetic: 5.25 us -> 0 us
  matrix products: 2.83 us -> 0 us
    psum x4 -> x0, blocking collectives: 58.4 us -> none  [the longest x2 34.8 us: row_totals(): return lax.psum(spread_rows(products), 'site')]
    pallas_call x0 -> x1, Pallas kernels: none -> 35 us  [local(): pl.pallas_call(functools.partial(kernel, npix, nsite), out_shape=(jax.Sha...]
    all_to_all x2 -> x0, waiting for transfers between devices: 15.1 us -> none  [the longest x1 15.1 us: local(): lax.all_to_all(coverage, 'pix', split_axis=0, concat_axis=0, tiled=True)]
    all_to_all x2 -> x0, starting transfers between devices: 9.51 us -> none  [the longest x1 5.17 us: local(): lax.all_to_all(position.astype(jnp.bfloat16), 'pix', split_axis=0, concat...]
    unnamed x18 -> x20, local copies, waits for them, and re-layouts: 0.09 us -> 8.88 us
    convert_element_type x5 -> x0, other arithmetic: 3.94 us -> none  [the longest x1 3.22 us: build_tiles(): return jnp.where(filled[:, None, None], values, 0.0).astype(jnp.bfloat16)]
    dot_general x9 -> x0, matrix products: 2.83 us -> none  [the longest x1 0.91 us: build_tiles(): lax.dot_general(pattern_gain, chooser, (((0,), (1,)), ((), ())), precisio...]
  transfers between devices with their start and end apart: 2 -> 0, of which waited for: 1 -> 0; matrix products, arithmetic and copies ran while one was open for 6% -> 0% of each run, Pallas kernels for 0% -> 0%
where the time goes in v1:
time: 45.1 us; the launch traced here: 44.6 us
  Pallas kernels  35 us (78%)
  local copies, waits for them, and re-layouts  8.88 us (20%)
  between operations  0.65 us (1%)
    pallas_call x1, Pallas kernels, local(): pl.pallas_call(functools.partial(kernel, npix, nsite), out_shape=(jax.Sha...  35 us
    unnamed x20, local copies, waits for them, and re-layouts  8.88 us

profile of v1, /device:TPU:0, one launch (start us, length us, event | category | flops | bytes accessed | tf_op | source)
XLA Modules:
  0.0 44.6 jit_solution(7097903130467364070)
XLA Ops:
  0.6 0.7 %copy.12.pos_ref = s32[16,1]{1,0:T(8,128)S(1)} copy(s32[16,1]{0,1:T(1,128)} %param.10) | data formatting | bytes 128 | tf_op args[1]
  1.4 0.0 copy-start
  1.4 1.6 %copy-done = s32[16,256,128]{2,1,0:T(8,128)S(1)} copy-done((s32[16,256,128]{2,1,0:T(8,128)S(1)}, s32[16,256,128]{2,1,0:T(8,128)}, u32[]{:S(2)}) %copy-start) | copy-done | bytes 2097176
  3.0 0.0 copy-start.1
  3.0 0.7 %copy-done.1 = f32[16,256]{1,0:T(8,128)S(1)} copy-done((f32[16,256]{1,0:T(8,128)S(1)}, f32[16,256]{1,0:T(8,128)}, u32[]{:S(2)}) %copy-start.1) | copy-done | bytes 16408
  3.7 0.0 copy-start.2
  3.7 0.7 %copy-done.2 = f32[4096]{0:T(1024)S(1)} copy-done((f32[4096]{0:T(1024)S(1)}, f32[4096]{0:T(1024)}, u32[]{:S(2)}) %copy-start.2) | copy-done | bytes 16408
  4.4 0.0 copy-start.3
  4.4 0.7 %copy-done.3 = f32[4096]{0:T(1024)S(1)} copy-done((f32[4096]{0:T(1024)S(1)}, f32[4096]{0:T(1024)}, u32[]{:S(2)}) %copy-start.3) | copy-done | bytes 16408
  5.1 0.0 copy-start.4
  5.1 0.7 %copy-done.4 = f32[4096]{0:T(1024)S(1)} copy-done((f32[4096]{0:T(1024)S(1)}, f32[4096]{0:T(1024)}, u32[]{:S(2)}) %copy-start.4) | copy-done | bytes 16408
  5.8 0.0 copy-start.5
  5.8 0.7 %copy-done.5 = s32[128]{0:T(128)S(1)} copy-done((s32[128]{0:T(128)S(1)}, s32[128]{0:T(128)}, u32[]{:S(2)}) %copy-start.5) | copy-done | bytes 536
  6.5 0.0 copy-start.6
  6.5 0.7 %copy-done.6 = f32[128]{0:T(128)S(1)} copy-done((f32[128]{0:T(128)S(1)}, f32[128]{0:T(128)}, u32[]{:S(2)}) %copy-start.6) | copy-done | bytes 536
  7.1 0.0 copy-start.7
  7.1 0.7 %copy-done.7 = f32[128]{0:T(128)S(1)} copy-done((f32[128]{0:T(128)S(1)}, f32[128]{0:T(128)}, u32[]{:S(2)}) %copy-start.7) | copy-done | bytes 536
  7.8 35.0 %shard_map.112 = (f32[1,128]{1,0:T(1,128)S(1)}, f32[32,128]{1,0:T(8,128)S(1)}, f32[32,128]{1,0:T(8,128)S(1)}) custom-call(s32[16,256,128]{2,1,0:T(8,128)S(1)} %copy-done, s32[16,1]{1,0:T(8,128)S(1)} %copy.12.pos_ref, s32[1,128]{1,0:T(1,128)S(1)} %bitcast.14, f32[16,256]{1,0:T(8,128)S(1)} %copy-done.1, f32[1,128]{1,0:T(1,128)S(1)} %bitcast.15, ...), custom_call_target="tpu_custom_call" | custom-call | tf_op jit(solution)/shard_map/pallas_call | solution.py:294
  42.8 0.5 %copy.16 = f32[128]{0:T(128)} copy(f32[128]{0:T(128)S(1)} %bitcast.17) | data formatting | bytes 1024
  43.3 0.6 %copy.17 = f32[4096]{0:T(1024)} copy(f32[4096]{0:T(1024)S(1)} %bitcast.13) | data formatting | bytes 32768
  43.9 0.6 %copy.18 = f32[4096]{0:T(1024)} copy(f32[4096]{0:T(1024)S(1)} %bitcast.12) | data formatting | bytes 32768
Async XLA Ops:
  1.4 1.6 %copy-start = (s32[16,256,128]{2,1,0:T(8,128)S(1)}, s32[16,256,128]{2,1,0:T(8,128)}, u32[]{:S(2)}) copy-start(s32[16,256,128]{2,1,0:T(8,128)} %margins_ref.1) | copy-start | bytes 6291460
  3.0 0.7 %copy-start.1 = (f32[16,256]{1,0:T(8,128)S(1)}, f32[16,256]{1,0:T(8,128)}, u32[]{:S(2)}) copy-start(f32[16,256]{1,0:T(8,128)} %gain_ref.1) | copy-start | bytes 49156
  3.7 0.7 %copy-start.2 = (f32[4096]{0:T(1024)S(1)}, f32[4096]{0:T(1024)}, u32[]{:S(2)}) copy-start(f32[4096]{0:T(1024)} %param.14) | copy-start | bytes 49156
  4.4 0.7 %copy-start.3 = (f32[4096]{0:T(1024)S(1)}, f32[4096]{0:T(1024)}, u32[]{:S(2)}) copy-start(f32[4096]{0:T(1024)} %param.16) | copy-start | bytes 49156
  5.1 0.7 %copy-start.4 = (f32[4096]{0:T(1024)S(1)}, f32[4096]{0:T(1024)}, u32[]{:S(2)}) copy-start(f32[4096]{0:T(1024)} %param.17) | copy-start | bytes 49156
  5.8 0.7 %copy-start.5 = (s32[128]{0:T(128)S(1)}, s32[128]{0:T(128)}, u32[]{:S(2)}) copy-start(s32[128]{0:T(128)} %param.11) | copy-start | bytes 1540
  6.5 0.7 %copy-start.6 = (f32[128]{0:T(128)S(1)}, f32[128]{0:T(128)}, u32[]{:S(2)}) copy-start(f32[128]{0:T(128)} %param.13) | copy-start | bytes 1540
  7.1 0.7 %copy-start.7 = (f32[128]{0:T(128)S(1)}, f32[128]{0:T(128)}, u32[]{:S(2)}) copy-start(f32[128]{0:T(128)} %param.15) | copy-start | bytes 1540

commit v2 on v1

v2 whole, which is shorter than its diff:
```python
import functools

import jax
import jax.numpy as jnp
from jax import lax
from jax.experimental import pallas as pl
from jax.experimental.pallas import tpu as pltpu
from jax.sharding import PartitionSpec as P

ITERS = 2
MARGIN_SCALE = 2.0 ** (-9)
LANES = 128
MESH = pl.DeviceIdType.MESH


def kernel(
    npix,
    nsite,
    margins_hbm,
    pos_hbm,
    ids_hbm,
    gain_hbm,
    price_hbm,
    weights_hbm,
    site_hbm,
    pixel_hbm,
    dual_hbm,
    site_hbm_out,
    pixel_hbm_out,
    dual_hbm_out,
    site_out,
    pixel_out,
    dual_out,
    margins_v,
    pos_ref,
    ids_ref,
    gain_ref,
    price_ref,
    weights_ref,
    site_ref,
    pixel_ref,
    dual_ref,
    tiles,
    tiles_t,
    dual_all,
    row_send,
    row_recv,
    col_recv,
    push_send,
    push_recv,
    margin_sem,
    small_sem,
    dual_sem,
    row_sem,
    col_sem,
    push_sem,
):
    slots, width, sites = margins_v.shape
    cap = slots // npix
    halves = width // LANES
    rows = dual_ref.shape[0]
    me = lax.axis_index("pix")
    here = lax.axis_index("site")
    mine = here * npix + me

    def pix_peer(step):
        return lax.rem(me + step, npix)

    def site_peer(step):
        return lax.rem(here + step, nsite)

    peers = [(p, z) for z in range(nsite) for p in range(npix) if p or z]

    small = [
        pltpu.make_async_copy(src, dst, small_sem.at[n])
        for n, (src, dst) in enumerate(
            (
                (dual_hbm, dual_ref),
                (pos_hbm, pos_ref),
                (ids_hbm, ids_ref),
                (gain_hbm, gain_ref),
                (price_hbm, price_ref),
                (weights_hbm, weights_ref),
                (site_hbm, site_ref),
                (pixel_hbm, pixel_ref),
            )
        )
    ]

    def margin_copy(t):
        part = pl.ds(t * cap, cap)
        return pltpu.make_async_copy(margins_hbm.at[part], margins_v.at[part], margin_sem.at[t])

    for copy in small:
        copy.start()
    for t in range(npix):
        margin_copy(t).start()

    barrier = pltpu.get_barrier_semaphore()
    for p, z in peers:
        pl.semaphore_signal(
            barrier, inc=1, device_id=(pix_peer(p), site_peer(z)), device_id_type=MESH
        )

    def send(src, dst, sems, p, z):
        pltpu.make_async_remote_copy(
            src_ref=src,
            dst_ref=dst,
            send_sem=sems.at[0],
            recv_sem=sems.at[1],
            device_id=(pix_peer(p), site_peer(z)),
            device_id_type=MESH,
        ).start()

    def drain(buffer, sem):
        part = buffer.at[pl.ds(0, buffer.shape[0] - 1)]
        pltpu.make_async_copy(part, part, sem).wait()

    def share_duals(i, values):
        dual_all[i, pl.ds(me, 1)] = values.astype(jnp.bfloat16)[None]

    def send_duals(i):
        for p in range(1, npix):
            send(dual_all.at[i, me], dual_all.at[i, me], dual_sem.at[i], p, 0)

    for copy in small:
        copy.wait()
    share_duals(0, dual_ref[...])

    diagonal = lax.broadcasted_iota(jnp.int32, (slots, slots), 0) == lax.broadcasted_iota(
        jnp.int32, (slots, slots), 1
    )
    pos = jnp.sum(
        jnp.where(diagonal, pos_ref[...].astype(jnp.float32), 0.0), axis=1, keepdims=True
    )
    slot_col = lax.broadcasted_iota(jnp.int32, (slots, 1), 0)
    first = ((slot_col // cap) * rows).astype(jnp.float32)
    base = jnp.where(pos >= 0.0, first + pos * halves, -1.0 * halves)
    row_id = lax.broadcasted_iota(jnp.int32, (slots, npix * rows), 1).astype(jnp.float32)
    choosers = [
        jnp.where(row_id == base + h, 1.0, 0.0).astype(jnp.bfloat16) for h in range(halves)
    ]
    pos_rows = jnp.broadcast_to(pos, (slots, LANES))
    for t in range(npix):
        row_send[t, halves * cap :, :] = pos_rows[t * cap : (t + 1) * cap]
    filled = jnp.broadcast_to(jnp.where(pos >= 0.0, 1.0, 0.0), (slots, width))
    slot_row = lax.broadcasted_iota(jnp.int32, (slots, width), 0) // cap
    slot_lane = lax.broadcasted_iota(jnp.int32, (slots, LANES), 0) % cap

    def of_target(t, values):
        return jnp.where(slot_row == t, values, 0.0).astype(jnp.bfloat16)

    def column_fold(sums):
        total = jnp.zeros((1, LANES), jnp.float32)
        for c in range(cap):
            part = sums[:, c * LANES : (c + 1) * LANES]
            total = total + jnp.sum(jnp.where(slot_lane == c, part, 0.0), axis=0, keepdims=True)
        return total

    lane_row = lax.broadcasted_iota(jnp.int32, (16, cap * LANES), 0)
    lane_cap = lax.broadcasted_iota(jnp.int32, (16, cap * LANES), 1) // LANES

    def spread_sites(values):
        wide = jnp.concatenate([values] * cap, axis=1)
        return jnp.where(lane_row == lane_cap, wide, 0.0).astype(jnp.bfloat16)

    chooser = (
        lax.broadcasted_iota(jnp.int32, (gain_ref.shape[0], sites), 0) == ids_ref[...]
    ).astype(jnp.float32)
    gain_half = 0.5 * lax.dot_general(
        gain_ref[...],
        chooser,
        (((0,), (0,)), ((), ())),
        precision=lax.Precision.HIGHEST,
        preferred_element_type=jnp.float32,
    )

    pl.semaphore_wait(barrier, len(peers))
    send_duals(0)

    def build(t, carry):
        margin_copy(t).wait()
        for c in range(cap):
            part = slice(c * LANES, (c + 1) * LANES)
            values = margins_v[t * cap + c].astype(jnp.float32)
            values = 0.5 * jnp.tanh(values * (0.5 * MARGIN_SCALE) + gain_half) + 0.5
            values = values.astype(jnp.bfloat16)
            tiles[t, :, part] = values
            tiles_t[t, part, :] = values.T
        return carry

    lax.fori_loop(0, npix, build, 0)

    def send_products(values, source, target, sems):
        lhs = spread_sites(values)
        for t in range(npix):
            products = jnp.dot(lhs, tiles_t[t], preferred_element_type=jnp.float32)
            for h in range(halves):
                source[t, h * cap : (h + 1) * cap, :] = products[
                    :cap, h * LANES : (h + 1) * LANES
                ]
        for p, z in peers:
            send(source.at[pix_peer(p)], target.at[mine], sems, p, z)
        target[pl.ds(mine, 1)] = source[pl.ds(me, 1)]

    state_row = lax.broadcasted_iota(jnp.int32, (rows, LANES), 0).astype(jnp.float32)

    def gather_rows(buffer):
        def group(z, total):
            for p in range(npix):
                s = z * npix + p
                for c in range(cap):
                    line = row_recv[s, halves * cap + c : halves * cap + c + 1, :]
                    offset = state_row - line * halves
                    for h in range(halves):
                        line = buffer[s, h * cap + c : h * cap + c + 1, :]
                        total = total + jnp.where(offset == h, line, 0.0)
            return total

        return lax.fori_loop(0, nsite, group, jnp.zeros((rows, LANES), jnp.float32))

    site_level = site_ref[...]
    pixel_level = pixel_ref[...]
    duals = dual_ref[...]
    column_sum = None
    row_sum = None
    for i in range(ITERS):
        drain(dual_all.at[i], dual_sem.at[i, 1])
        all_rows = dual_all[i].reshape(npix * rows, LANES)
        selected = jnp.concatenate(
            [jnp.dot(ch, all_rows, preferred_element_type=jnp.float32) for ch in choosers], axis=1
        )
        groups = [selected, filled] if i == 0 else [selected]
        sums = jnp.zeros((len(groups) * slots, cap * LANES), jnp.float32)
        for t in range(npix):
            lhs = jnp.concatenate([of_target(t, group) for group in groups], axis=0)
            sums = sums + jnp.dot(lhs, tiles[t], preferred_element_type=jnp.float32)
        for n in range(len(groups)):
            total = column_fold(sums[n * slots : (n + 1) * slots])
            col_recv[i, pl.ds(me, 1), n : n + 1] = total[None]
        for p in range(1, npix):
            send(col_recv.at[i, me], col_recv.at[i, me], col_sem.at[i], p, 0)

        new_pixel = jnp.clip(pixel_level - (duals - weights_ref[...]), 0.0, 1.0)
        ahead = 2.0 * new_pixel - pixel_level
        if i == 0:
            send_products(jnp.ones((1, LANES), jnp.float32), row_send, row_recv, row_sem)

        drain(col_recv.at[i], col_sem.at[i, 1])
        pulled = col_recv[i, 0]
        for s in range(1, npix):
            pulled = pulled + col_recv[i, s]
        if i == 0:
            column_sum = pulled[1:2]
        new_site = jnp.clip(site_level - (price_ref[...] - pulled[0:1] / column_sum), 0.0, 1.0)
        send_products(
            2.0 * new_site - site_level, push_send.at[i], push_recv.at[i], push_sem.at[i]
        )
        if i == 0:
            drain(row_recv, row_sem.at[1])
            row_sum = gather_rows(row_recv) + 1.0
        drain(push_recv.at[i], push_sem.at[i, 1])
        pushed = gather_rows(push_recv.at[i])
        duals = jnp.maximum(duals + (ahead - pushed) / row_sum, 0.0)
        if i < ITERS - 1:
            share_duals(i + 1, duals)
            send_duals(i + 1)
        site_level, pixel_level = new_site, new_pixel

    site_out[...] = site_level
    pixel_out[...] = pixel_level
    dual_out[...] = duals
    write_out(
        site_out, pixel_out, dual_out, site_hbm_out, pixel_hbm_out, dual_hbm_out, small_sem
    )

    drain(row_recv, row_sem.at[0])
    for i in range(ITERS):
        drain(dual_all.at[i], dual_sem.at[i, 0])
        drain(col_recv.at[i], col_sem.at[i, 0])
        drain(push_recv.at[i], push_sem.at[i, 0])


def write_out(site_in, pixel_in, dual_in, site_out, pixel_out, dual_out, sem):
    copies = [
        pltpu.make_async_copy(src, dst, sem.at[n])
        for n, (src, dst) in enumerate(
            ((site_in, site_out), (pixel_in, pixel_out), (dual_in, dual_out))
        )
    ]
    for copy in copies:
        copy.start()
    for copy in copies:
        copy.wait()


def local(
    npix,
    nsite,
    margins,
    block_pos,
    pattern_ids,
    pattern_gain,
    site_price,
    weights,
    site_start,
    pixel_start,
    dual_start,
):
    slots, width, sites = margins.shape
    cap = slots // npix
    halves = width // LANES
    rows = weights.shape[0] // LANES
    devices = npix * nsite
    f32 = jnp.float32
    i32 = jnp.int32
    hbm = pl.BlockSpec(memory_space=pltpu.HBM)
    dma = pltpu.SemaphoreType.DMA
    results = (
        jax.ShapeDtypeStruct((1, sites), f32),
        jax.ShapeDtypeStruct((rows, LANES), f32),
        jax.ShapeDtypeStruct((rows, LANES), f32),
    )
    found = pl.pallas_call(
        functools.partial(kernel, npix, nsite),
        out_shape=results,
        in_specs=[hbm] * 9,
        out_specs=(hbm, hbm, hbm),
        scratch_shapes=[
            pltpu.VMEM((1, sites), f32),
            pltpu.VMEM((rows, LANES), f32),
            pltpu.VMEM((rows, LANES), f32),
            pltpu.VMEM((slots, width, sites), i32),
            pltpu.VMEM((1, slots), i32),
            pltpu.VMEM((1, sites), i32),
            pltpu.VMEM(pattern_gain.shape, f32),
            pltpu.VMEM((1, sites), f32),
            pltpu.VMEM((rows, LANES), f32),
            pltpu.VMEM((1, sites), f32),
            pltpu.VMEM((rows, LANES), f32),
            pltpu.VMEM((rows, LANES), f32),
            pltpu.VMEM((npix, width, cap * sites), jnp.bfloat16),
            pltpu.VMEM((npix, cap * sites, width), jnp.bfloat16),
            pltpu.VMEM((ITERS, npix, rows, LANES), jnp.bfloat16),
            pltpu.VMEM((npix, (halves + 1) * cap, LANES), f32),
            pltpu.VMEM((devices, (halves + 1) * cap, LANES), f32),
            pltpu.VMEM((ITERS, npix, 2, LANES), f32),
            pltpu.VMEM((ITERS, npix, halves * cap, LANES), f32),
            pltpu.VMEM((ITERS, devices, halves * cap, LANES), f32),
            dma((npix,)),
            dma((8,)),
            dma((ITERS, 2)),
            dma((2,)),
            dma((ITERS, 2)),
            dma((ITERS, 2)),
        ],
        compiler_params=pltpu.CompilerParams(
            collective_id=0, has_side_effects=True, vmem_limit_bytes=60 * 1024 * 1024
        ),
    )(
        margins,
        block_pos.reshape(1, slots),
        pattern_ids.reshape(1, sites),
        pattern_gain,
        site_price.reshape(1, sites),
        weights.reshape(rows, LANES),
        site_start.reshape(1, sites),
        pixel_start.reshape(rows, LANES),
        dual_start.reshape(rows, LANES),
    )
    site_level, pixel_level, duals = pl.pallas_call(
        write_out,
        out_shape=results,
        in_specs=[hbm] * 3,
        out_specs=(hbm, hbm, hbm),
        scratch_shapes=[dma((3,))],
        compiler_params=pltpu.CompilerParams(vmem_limit_bytes=60 * 1024 * 1024),
    )(*found)
    return site_level.reshape(-1), pixel_level.reshape(-1), duals.reshape(-1)


def solution(mesh):
    placed = (
        P("pix", None, "site"),
        P("pix", "site"),
        P("site"),
        P(),
        P("site"),
        P("pix"),
        P("site"),
        P("pix"),
        P("pix"),
    )
    return jax.shard_map(
        functools.partial(local, mesh.shape["pix"], mesh.shape["site"]),
        mesh=mesh,
        in_specs=placed,
        out_specs=(P("site"), P("pix"), P("pix")),
        check_vma=False,
    )
```

time: 45.1 us -> 34.9 us (0.77)
  local copies, waits for them, and re-layouts: 8.88 us -> 0 us
  Pallas kernels: 35 us -> 34 us
    unnamed x20 -> x0, local copies, waits for them, and re-layouts: 8.88 us -> none
    pallas_call x1 -> x2, Pallas kernels: 35 us -> 34 us  [the longest x1 31.9 us: local(): pl.pallas_call(functools.partial(kernel, npix, nsite), out_shape=results,...]
where the time goes in v2:
time: 34.9 us; the launch traced here: 34.6 us
  Pallas kernels  34 us (97%)
  between operations  0.64 us (2%)
    pallas_call x1, Pallas kernels, local(): pl.pallas_call(functools.partial(kernel, npix, nsite), out_shape=results,...  31.9 us
    pallas_call x1, Pallas kernels, local(): pl.pallas_call(write_out, out_shape=results, in_specs=[hbm] * 3, out_spec...  2.14 us

profile of v2, /device:TPU:0, one launch (start us, length us, event | category | flops | bytes accessed | tf_op | source)
XLA Modules:
  0.0 34.6 jit_solution(4600807863345536921)
XLA Ops:
  0.6 31.9 %shard_map.112 = (f32[1,128]{1,0:T(1,128)}, f32[32,128]{1,0:T(8,128)}, f32[32,128]{1,0:T(8,128)}) custom-call(s32[16,256,128]{2,1,0:T(8,128)} %margins_hbm.1, s32[1,16]{1,0:T(1,128)} %bitcast.13, s32[1,128]{1,0:T(1,128)} %bitcast.14, f32[16,256]{1,0:T(8,128)} %gain_hbm.1, f32[1,128]{1,0:T(1,128)} %bitcast.15, f32[32,128]{1,0:T(8,128)} %bitcast.10, ...), custom_call_target="tpu_custom_call" | custom-call | tf_op jit(solution)/shard_map/pallas_call | solution.py:324
  32.5 2.1 %shard_map.113 = (f32[1,128]{1,0:T(1,128)}, f32[32,128]{1,0:T(8,128)}, f32[32,128]{1,0:T(8,128)}) custom-call(f32[1,128]{1,0:T(1,128)} %get-tuple-element.9.site_in, f32[32,128]{1,0:T(8,128)} %get-tuple-element.10.pixel_in, f32[32,128]{1,0:T(8,128)} %get-tuple-element.11.dual_in), custom_call_target="tpu_custom_call" | custom-call | tf_op jit(solution)/shard_map/pallas_call | solution.py:371

commit v3 on v2

--- a/solution.py
+++ b/solution.py
@@ -48,9 +48,13 @@
     col_recv,
     push_send,
     push_recv,
+    tiles_recv,
+    level_recv,
     margin_sem,
     small_sem,
     dual_sem,
+    tile_sem,
+    level_sem,
     row_sem,
     col_sem,
     push_sem,
@@ -69,7 +73,8 @@
     def site_peer(step):
         return lax.rem(here + step, nsite)
 
-    peers = [(p, z) for z in range(nsite) for p in range(npix) if p or z]
+    far_first = sorted(range(nsite), key=lambda z: -min(z, nsite - z))
+    peers = [(p, z) for z in far_first for p in range(npix) if p or z]
 
     small = [
         pltpu.make_async_copy(src, dst, small_sem.at[n])
@@ -116,16 +121,9 @@
         part = buffer.at[pl.ds(0, buffer.shape[0] - 1)]
         pltpu.make_async_copy(part, part, sem).wait()
 
-    def share_duals(i, values):
-        dual_all[i, pl.ds(me, 1)] = values.astype(jnp.bfloat16)[None]
-
-    def send_duals(i):
-        for p in range(1, npix):
-            send(dual_all.at[i, me], dual_all.at[i, me], dual_sem.at[i], p, 0)
-
     for copy in small:
         copy.wait()
-    share_duals(0, dual_ref[...])
+    dual_all[pl.ds(me, 1)] = dual_ref[...].astype(jnp.bfloat16)[None]
 
     diagonal = lax.broadcasted_iota(jnp.int32, (slots, slots), 0) == lax.broadcasted_iota(
         jnp.int32, (slots, slots), 1
@@ -176,9 +174,10 @@
     )
 
     pl.semaphore_wait(barrier, len(peers))
-    send_duals(0)
-
-    def build(t, carry):
+    for p in range(1, npix):
+        send(dual_all.at[me], dual_all.at[me], dual_sem, p, 0)
+
+    def build(t):
         margin_copy(t).wait()
         for c in range(cap):
             part = slice(c * LANES, (c + 1) * LANES)
@@ -187,11 +186,18 @@
             values = values.astype(jnp.bfloat16)
             tiles[t, :, part] = values
             tiles_t[t, part, :] = values.T
+
+    def build_and_send(step, carry):
+        t = pix_peer(step)
+        build(t)
+        send(tiles.at[t], tiles_recv.at[me], tile_sem, step, 0)
         return carry
 
-    lax.fori_loop(0, npix, build, 0)
-
-    def send_products(values, source, target, sems):
+    lax.fori_loop(1, npix, build_and_send, 0)
+    build(me)
+    tiles_recv[pl.ds(me, 1)] = tiles[pl.ds(me, 1)]
+
+    def fill_products(values, source):
         lhs = spread_sites(values)
         for t in range(npix):
             products = jnp.dot(lhs, tiles_t[t], preferred_element_type=jnp.float32)
@@ -199,52 +205,74 @@
                 source[t, h * cap : (h + 1) * cap, :] = products[
                     :cap, h * LANES : (h + 1) * LANES
                 ]
+
+    def send_products(values, source, target, sems):
+        fill_products(values, source)
         for p, z in peers:
             send(source.at[pix_peer(p)], target.at[mine], sems, p, z)
         target[pl.ds(mine, 1)] = source[pl.ds(me, 1)]
 
     state_row = lax.broadcasted_iota(jnp.int32, (rows, LANES), 0).astype(jnp.float32)
 
+    def gather_group(z, buffer, first_line, total):
+        for p in range(npix):
+            s = z * npix + p
+            for c in range(cap):
+                line = row_recv[s, halves * cap + c : halves * cap + c + 1, :]
+                offset = state_row - line * halves
+                for h in range(halves):
+                    line = buffer[first_line + p, h * cap + c : h * cap + c + 1, :]
+                    total = total + jnp.where(offset == h, line, 0.0)
+        return total
+
+    no_rows = jnp.zeros((rows, LANES), jnp.float32)
+
     def gather_rows(buffer):
         def group(z, total):
-            for p in range(npix):
-                s = z * npix + p
-                for c in range(cap):
-                    line = row_recv[s, halves * cap + c : halves * cap + c + 1, :]
-                    offset = state_row - line * halves
-                    for h in range(halves):
-                        line = buffer[s, h * cap + c : h * cap + c + 1, :]
-                        total = total + jnp.where(offset == h, line, 0.0)
-            return total
-
-        return lax.fori_loop(0, nsite, group, jnp.zeros((rows, LANES), jnp.float32))
+            return gather_group(z, buffer, z * npix, total)
+
+        return lax.fori_loop(0, nsite, group, no_rows)
+
+    def column_totals(picked, groups, source):
+        sums = jnp.zeros((len(groups) * slots, cap * LANES), jnp.float32)
+        for t in range(npix):
+            lhs = jnp.concatenate([of_target(t, group) for group in groups], axis=0)
+            sums = sums + jnp.dot(lhs, source[t], preferred_element_type=jnp.float32)
+        for n in range(len(groups)):
+            total = column_fold(sums[n * slots : (n + 1) * slots])
+            col_recv[picked, pl.ds(me, 1), n : n + 1] = total[None]
+        for p in range(1, npix):
+            send(col_recv.at[picked, me], col_recv.at[picked, me], col_sem.at[picked], p, 0)
+
+    def pick(ch, values):
+        return jnp.concatenate(
+            [jnp.dot(c, values, preferred_element_type=jnp.float32) for c in ch], axis=1
+        )
 
     site_level = site_ref[...]
     pixel_level = pixel_ref[...]
     duals = dual_ref[...]
     column_sum = None
     row_sum = None
+    own_choosers = None
     for i in range(ITERS):
-        drain(dual_all.at[i], dual_sem.at[i, 1])
-        all_rows = dual_all[i].reshape(npix * rows, LANES)
-        selected = jnp.concatenate(
-            [jnp.dot(ch, all_rows, preferred_element_type=jnp.float32) for ch in choosers], axis=1
-        )
-        groups = [selected, filled] if i == 0 else [selected]
-        sums = jnp.zeros((len(groups) * slots, cap * LANES), jnp.float32)
-        for t in range(npix):
-            lhs = jnp.concatenate([of_target(t, group) for group in groups], axis=0)
-            sums = sums + jnp.dot(lhs, tiles[t], preferred_element_type=jnp.float32)
-        for n in range(len(groups)):
-            total = column_fold(sums[n * slots : (n + 1) * slots])
-            col_recv[i, pl.ds(me, 1), n : n + 1] = total[None]
-        for p in range(1, npix):
-            send(col_recv.at[i, me], col_recv.at[i, me], col_sem.at[i], p, 0)
+        if i == 0:
+            drain(dual_all, dual_sem.at[1])
+            selected = pick(choosers, dual_all[...].reshape(npix * rows, LANES))
+            column_totals(i, [selected, filled], tiles)
+        else:
+            selected = pick(own_choosers, duals.astype(jnp.bfloat16))
+            if i == 1:
+                drain(tiles_recv, tile_sem.at[1])
+            column_totals(i, [selected], tiles_recv)
 
         new_pixel = jnp.clip(pixel_level - (duals - weights_ref[...]), 0.0, 1.0)
         ahead = 2.0 * new_pixel - pixel_level
         if i == 0:
             send_products(jnp.ones((1, LANES), jnp.float32), row_send, row_recv, row_sem)
+        if i == 1:
+            for t in range(npix):
+                tiles_t[t] = tiles_recv[t].T
 
         drain(col_recv.at[i], col_sem.at[i, 1])
         pulled = col_recv[i, 0]
@@ -253,45 +281,74 @@
         if i == 0:
             column_sum = pulled[1:2]
         new_site = jnp.clip(site_level - (price_ref[...] - pulled[0:1] / column_sum), 0.0, 1.0)
-        send_products(
-            2.0 * new_site - site_level, push_send.at[i], push_recv.at[i], push_sem.at[i]
-        )
+        ahead_sites = 2.0 * new_site - site_level
         if i == 0:
+            send_products(ahead_sites, push_send, push_recv, push_sem)
             drain(row_recv, row_sem.at[1])
             row_sum = gather_rows(row_recv) + 1.0
-        drain(push_recv.at[i], push_sem.at[i, 1])
-        pushed = gather_rows(push_recv.at[i])
+            arrived = jnp.concatenate(
+                [
+                    row_recv[here * npix + s, halves * cap : (halves + 1) * cap, :rows]
+                    for s in range(npix)
+                ],
+                axis=0,
+            )
+            own_row = lax.broadcasted_iota(jnp.int32, (slots, rows), 1).astype(jnp.float32)
+            own_choosers = [
+                jnp.where(own_row == arrived * halves + h, 1.0, 0.0).astype(jnp.bfloat16)
+                for h in range(halves)
+            ]
+            drain(push_recv, push_sem.at[1])
+            pushed = gather_rows(push_recv)
+        else:
+            if i == 1:
+                drain(push_recv, push_sem.at[0])
+            fill_products(ahead_sites, push_send)
+            level = level_recv.at[i - 1]
+            level[pl.ds(here, 1)] = gather_group(here, push_send, 0, no_rows)[None]
+            for z in far_first:
+                if z:
+                    send(level.at[here], level.at[here], level_sem.at[i - 1], 0, z)
+            drain(level, level_sem.at[i - 1, 1])
+            pushed = level[0]
+            for z in range(1, nsite):
+                pushed = pushed + level[z]
         duals = jnp.maximum(duals + (ahead - pushed) / row_sum, 0.0)
-        if i < ITERS - 1:
-            share_duals(i + 1, duals)
-            send_duals(i + 1)
         site_level, pixel_level = new_site, new_pixel
 
     site_out[...] = site_level
     pixel_out[...] = pixel_level
     dual_out[...] = duals
-    write_out(
-        site_out, pixel_out, dual_out, site_hbm_out, pixel_hbm_out, dual_hbm_out, small_sem
+    move_all(
+        (site_out, pixel_out, dual_out),
+        (site_hbm_out, pixel_hbm_out, dual_hbm_out),
+        small_sem,
     )
 
     drain(row_recv, row_sem.at[0])
+    drain(dual_all, dual_sem.at[0])
+    drain(tiles_recv, tile_sem.at[0])
     for i in range(ITERS):
-        drain(dual_all.at[i], dual_sem.at[i, 0])
         drain(col_recv.at[i], col_sem.at[i, 0])
-        drain(push_recv.at[i], push_sem.at[i, 0])
-
-
-def write_out(site_in, pixel_in, dual_in, site_out, pixel_out, dual_out, sem):
+    for i in range(ITERS - 1):
+        drain(level_recv.at[i], level_sem.at[i, 0])
+
+
+def move_all(sources, targets, sem):
     copies = [
         pltpu.make_async_copy(src, dst, sem.at[n])
-        for n, (src, dst) in enumerate(
-            ((site_in, site_out), (pixel_in, pixel_out), (dual_in, dual_out))
-        )
+        for n, (src, dst) in enumerate(zip(sources, targets))
     ]
     for copy in copies:
         copy.start()
     for copy in copies:
         copy.wait()
+
+
+def hand_on(site_in, pixel_in, dual_in, site_out, pixel_out, dual_out, site, pixel, dual, sem):
+    held = (site, pixel, dual)
+    move_all((site_in, pixel_in, dual_in), held, sem)
+    move_all(held, (site_out, pixel_out, dual_out), sem)
 
 
 def local(
@@ -341,18 +398,22 @@
             pltpu.VMEM((rows, LANES), f32),
             pltpu.VMEM((npix, width, cap * sites), jnp.bfloat16),
             pltpu.VMEM((npix, cap * sites, width), jnp.bfloat16),
-            pltpu.VMEM((ITERS, npix, rows, LANES), jnp.bfloat16),
+            pltpu.VMEM((npix, rows, LANES), jnp.bfloat16),
             pltpu.VMEM((npix, (halves + 1) * cap, LANES), f32),
             pltpu.VMEM((devices, (halves + 1) * cap, LANES), f32),
             pltpu.VMEM((ITERS, npix, 2, LANES), f32),
-            pltpu.VMEM((ITERS, npix, halves * cap, LANES), f32),
-            pltpu.VMEM((ITERS, devices, halves * cap, LANES), f32),
+            pltpu.VMEM((npix, halves * cap, LANES), f32),
+            pltpu.VMEM((devices, halves * cap, LANES), f32),
+            pltpu.VMEM((npix, width, cap * sites), jnp.bfloat16),
+            pltpu.VMEM((ITERS - 1, nsite, rows, LANES), f32),
             dma((npix,)),
             dma((8,)),
+            dma((2,)),
+            dma((2,)),
+            dma((ITERS - 1, 2)),
+            dma((2,)),
             dma((ITERS, 2)),
             dma((2,)),
-            dma((ITERS, 2)),
-            dma((ITERS, 2)),
         ],
         compiler_params=pltpu.CompilerParams(
             collective_id=0, has_side_effects=True, vmem_limit_bytes=60 * 1024 * 1024
@@ -369,11 +430,11 @@
         dual_start.reshape(rows, LANES),
     )
     site_level, pixel_level, duals = pl.pallas_call(
-        write_out,
+        hand_on,
         out_shape=results,
         in_specs=[hbm] * 3,
         out_specs=(hbm, hbm, hbm),
-        scratch_shapes=[dma((3,))],
+        scratch_shapes=[pltpu.VMEM(r.shape, f32) for r in results] + [dma((3,))],
         compiler_params=pltpu.CompilerParams(vmem_limit_bytes=60 * 1024 * 1024),
     )(*found)
     return site_level.reshape(-1), pixel_level.reshape(-1), duals.reshape(-1)

time: 34.9 us -> 37.9 us (1.086)
  Pallas kernels: 34 us -> 37 us
    pallas_call x1, Pallas kernels: 31.9 us -> 35.6 us  [local(): pl.pallas_call(functools.partial(kernel, npix, nsite), out_shape=results,...]
    pallas_call x1, Pallas kernels: 2.14 us -> 1.38 us  [local(): pl.pallas_call(hand_on, out_shape=results, in_specs=[hbm] * 3, out_specs=...]
where the time goes in v3:
time: 37.9 us; the launch traced here: 37.6 us
  Pallas kernels  37 us (98%)
  between operations  0.64 us (2%)
    pallas_call x1, Pallas kernels, local(): pl.pallas_call(functools.partial(kernel, npix, nsite), out_shape=results,...  35.6 us
    pallas_call x1, Pallas kernels, local(): pl.pallas_call(hand_on, out_shape=results, in_specs=[hbm] * 3, out_specs=...  1.38 us

profile of v3, /device:TPU:0, one launch (start us, length us, event | category | flops | bytes accessed | tf_op | source)
XLA Modules:
  0.0 37.6 jit_solution(7575510838543270684)
XLA Ops:
  0.6 35.6 %shard_map.112 = (f32[1,128]{1,0:T(1,128)}, f32[32,128]{1,0:T(8,128)}, f32[32,128]{1,0:T(8,128)}) custom-call(s32[16,256,128]{2,1,0:T(8,128)} %margins_hbm.1, s32[1,16]{1,0:T(1,128)} %bitcast.13, s32[1,128]{1,0:T(1,128)} %bitcast.14, f32[16,256]{1,0:T(8,128)} %gain_hbm.1, f32[1,128]{1,0:T(1,128)} %bitcast.15, f32[32,128]{1,0:T(8,128)} %bitcast.10, ...), custom_call_target="tpu_custom_call" | custom-call | tf_op jit(solution)/shard_map/pallas_call | solution.py:381
  36.2 1.4 %shard_map.113 = (f32[1,128]{1,0:T(1,128)}, f32[32,128]{1,0:T(8,128)}, f32[32,128]{1,0:T(8,128)}) custom-call(f32[1,128]{1,0:T(1,128)} %get-tuple-element.9.site_in, f32[32,128]{1,0:T(8,128)} %get-tuple-element.10.pixel_in, f32[32,128]{1,0:T(8,128)} %get-tuple-element.11.dual_in), custom_call_target="tpu_custom_call" | custom-call | tf_op jit(solution)/shard_map/pallas_call | solution.py:432

commit v4 on v2

--- a/solution.py
+++ b/solution.py
@@ -69,7 +69,8 @@
     def site_peer(step):
         return lax.rem(here + step, nsite)
 
-    peers = [(p, z) for z in range(nsite) for p in range(npix) if p or z]
+    far_first = sorted(range(nsite), key=lambda z: -min(z, nsite - z))
+    peers = [(p, z) for p in list(range(1, npix)) + [0] for z in far_first if p or z]
 
     small = [
         pltpu.make_async_copy(src, dst, small_sem.at[n])
@@ -186,21 +187,32 @@
             values = 0.5 * jnp.tanh(values * (0.5 * MARGIN_SCALE) + gain_half) + 0.5
             values = values.astype(jnp.bfloat16)
             tiles[t, :, part] = values
-            tiles_t[t, part, :] = values.T
         return carry
 
     lax.fori_loop(0, npix, build, 0)
 
-    def send_products(values, source, target, sems):
+    def send_products(values, source, target, sems, turn):
         lhs = spread_sites(values)
-        for t in range(npix):
-            products = jnp.dot(lhs, tiles_t[t], preferred_element_type=jnp.float32)
+        order = [pix_peer(p) for p in list(range(1, npix)) + [0]]
+
+        def multiply(t):
+            if turn:
+                tiles_t[t] = tiles[t].T
+            return jnp.dot(lhs, tiles_t[t], preferred_element_type=jnp.float32)
+
+        ready = multiply(order[0])
+        for n, t in enumerate(order):
+            products = ready
             for h in range(halves):
                 source[t, h * cap : (h + 1) * cap, :] = products[
                     :cap, h * LANES : (h + 1) * LANES
                 ]
-        for p, z in peers:
-            send(source.at[pix_peer(p)], target.at[mine], sems, p, z)
+            if n + 1 < npix:
+                ready = multiply(order[n + 1])
+            p = (n + 1) % npix
+            for z in far_first:
+                if p or z:
+                    send(source.at[t], target.at[mine], sems, p, z)
         target[pl.ds(mine, 1)] = source[pl.ds(me, 1)]
 
     state_row = lax.broadcasted_iota(jnp.int32, (rows, LANES), 0).astype(jnp.float32)
@@ -244,7 +256,7 @@
         new_pixel = jnp.clip(pixel_level - (duals - weights_ref[...]), 0.0, 1.0)
         ahead = 2.0 * new_pixel - pixel_level
         if i == 0:
-            send_products(jnp.ones((1, LANES), jnp.float32), row_send, row_recv, row_sem)
+            send_products(jnp.ones((1, LANES), jnp.float32), row_send, row_recv, row_sem, True)
 
         drain(col_recv.at[i], col_sem.at[i, 1])
         pulled = col_recv[i, 0]
@@ -254,7 +266,7 @@
             column_sum = pulled[1:2]
         new_site = jnp.clip(site_level - (price_ref[...] - pulled[0:1] / column_sum), 0.0, 1.0)
         send_products(
-            2.0 * new_site - site_level, push_send.at[i], push_recv.at[i], push_sem.at[i]
+            2.0 * new_site - site_level, push_send.at[i], push_recv.at[i], push_sem.at[i], False
         )
         if i == 0:
             drain(row_recv, row_sem.at[1])
@@ -270,8 +282,10 @@
     site_out[...] = site_level
     pixel_out[...] = pixel_level
     dual_out[...] = duals
-    write_out(
-        site_out, pixel_out, dual_out, site_hbm_out, pixel_hbm_out, dual_hbm_out, small_sem
+    move_all(
+        (site_out, pixel_out, dual_out),
+        (site_hbm_out, pixel_hbm_out, dual_hbm_out),
+        small_sem,
     )
 
     drain(row_recv, row_sem.at[0])
@@ -281,17 +295,21 @@
         drain(push_recv.at[i], push_sem.at[i, 0])
 
 
-def write_out(site_in, pixel_in, dual_in, site_out, pixel_out, dual_out, sem):
+def move_all(sources, targets, sem):
     copies = [
         pltpu.make_async_copy(src, dst, sem.at[n])
-        for n, (src, dst) in enumerate(
-            ((site_in, site_out), (pixel_in, pixel_out), (dual_in, dual_out))
-        )
+        for n, (src, dst) in enumerate(zip(sources, targets))
     ]
     for copy in copies:
         copy.start()
     for copy in copies:
         copy.wait()
+
+
+def hand_on(site_in, pixel_in, dual_in, site_out, pixel_out, dual_out, site, pixel, dual, sem):
+    held = (site, pixel, dual)
+    move_all((site_in, pixel_in, dual_in), held, sem)
+    move_all(held, (site_out, pixel_out, dual_out), sem)
 
 
 def local(
@@ -369,11 +387,11 @@
         dual_start.reshape(rows, LANES),
     )
     site_level, pixel_level, duals = pl.pallas_call(
-        write_out,
+        hand_on,
         out_shape=results,
         in_specs=[hbm] * 3,
         out_specs=(hbm, hbm, hbm),
-        scratch_shapes=[dma((3,))],
+        scratch_shapes=[pltpu.VMEM(r.shape, f32) for r in results] + [dma((3,))],
         compiler_params=pltpu.CompilerParams(vmem_limit_bytes=60 * 1024 * 1024),
     )(*found)
     return site_level.reshape(-1), pixel_level.reshape(-1), duals.reshape(-1)

time: 34.9 us -> 33.8 us (0.968)
  Pallas kernels: 34 us -> 32.9 us
    pallas_call x1, Pallas kernels: 2.14 us -> 1.38 us  [local(): pl.pallas_call(hand_on, out_shape=results, in_specs=[hbm] * 3, out_specs=...]
    pallas_call x1, Pallas kernels: 31.9 us -> 31.5 us  [local(): pl.pallas_call(functools.partial(kernel, npix, nsite), out_shape=results,...]
where the time goes in v4:
time: 33.8 us; the launch traced here: 33.5 us
  Pallas kernels  32.9 us (97%)
  between operations  0.64 us (2%)
    pallas_call x1, Pallas kernels, local(): pl.pallas_call(functools.partial(kernel, npix, nsite), out_shape=results,...  31.5 us
    pallas_call x1, Pallas kernels, local(): pl.pallas_call(hand_on, out_shape=results, in_specs=[hbm] * 3, out_specs=...  1.38 us

profile of v4, /device:TPU:0, one launch (start us, length us, event | category | flops | bytes accessed | tf_op | source)
XLA Modules:
  0.0 33.5 jit_solution(5872499650655645044)
XLA Ops:
  0.6 31.5 %shard_map.112 = (f32[1,128]{1,0:T(1,128)}, f32[32,128]{1,0:T(8,128)}, f32[32,128]{1,0:T(8,128)}) custom-call(s32[16,256,128]{2,1,0:T(8,128)} %margins_hbm.1, s32[1,16]{1,0:T(1,128)} %bitcast.13, s32[1,128]{1,0:T(1,128)} %bitcast.14, f32[16,256]{1,0:T(8,128)} %gain_hbm.1, f32[1,128]{1,0:T(1,128)} %bitcast.15, f32[32,128]{1,0:T(8,128)} %bitcast.10, ...), custom_call_target="tpu_custom_call" | custom-call | tf_op jit(solution)/shard_map/pallas_call | solution.py:342
  32.1 1.4 %shard_map.113 = (f32[1,128]{1,0:T(1,128)}, f32[32,128]{1,0:T(8,128)}, f32[32,128]{1,0:T(8,128)}) custom-call(f32[1,128]{1,0:T(1,128)} %get-tuple-element.9.site_in, f32[32,128]{1,0:T(8,128)} %get-tuple-element.10.pixel_in, f32[32,128]{1,0:T(8,128)} %get-tuple-element.11.dual_in), custom_call_target="tpu_custom_call" | custom-call | tf_op jit(solution)/shard_map/pallas_call | solution.py:389

commit v5 on v4

--- a/solution.py
+++ b/solution.py
@@ -70,7 +70,6 @@
         return lax.rem(here + step, nsite)
 
     far_first = sorted(range(nsite), key=lambda z: -min(z, nsite - z))
-    peers = [(p, z) for p in list(range(1, npix)) + [0] for z in far_first if p or z]
 
     small = [
         pltpu.make_async_copy(src, dst, small_sem.at[n])
@@ -94,14 +93,25 @@
 
     for copy in small:
         copy.start()
-    for t in range(npix):
+    @pl.loop(0, npix)
+    def start_margins(t):
         margin_copy(t).start()
 
     barrier = pltpu.get_barrier_semaphore()
-    for p, z in peers:
+
+    def greet(p, z):
         pl.semaphore_signal(
             barrier, inc=1, device_id=(pix_peer(p), site_peer(z)), device_id_type=MESH
         )
+
+    @pl.loop(1, npix)
+    def greet_all(p):
+        for z in far_first:
+            greet(p, z)
+
+    for z in far_first:
+        if z:
+            greet(0, z)
 
     def send(src, dst, sems, p, z):
         pltpu.make_async_remote_copy(
@@ -121,7 +131,8 @@
         dual_all[i, pl.ds(me, 1)] = values.astype(jnp.bfloat16)[None]
 
     def send_duals(i):
-        for p in range(1, npix):
+        @pl.loop(1, npix)
+        def send_all(p):
             send(dual_all.at[i, me], dual_all.at[i, me], dual_sem.at[i], p, 0)
 
     for copy in small:
@@ -176,7 +187,7 @@
         preferred_element_type=jnp.float32,
     )
 
-    pl.semaphore_wait(barrier, len(peers))
+    pl.semaphore_wait(barrier, npix * nsite - 1)
     send_duals(0)
 
     def build(t, carry):
@@ -193,26 +204,30 @@
 
     def send_products(values, source, target, sems, turn):
         lhs = spread_sites(values)
-        order = [pix_peer(p) for p in list(range(1, npix)) + [0]]
 
         def multiply(t):
             if turn:
                 tiles_t[t] = tiles[t].T
             return jnp.dot(lhs, tiles_t[t], preferred_element_type=jnp.float32)
 
-        ready = multiply(order[0])
-        for n, t in enumerate(order):
-            products = ready
+        def put(t, products):
             for h in range(halves):
                 source[t, h * cap : (h + 1) * cap, :] = products[
                     :cap, h * LANES : (h + 1) * LANES
                 ]
-            if n + 1 < npix:
-                ready = multiply(order[n + 1])
-            p = (n + 1) % npix
+
+        def go(p, ready):
+            t = pix_peer(p)
+            put(t, ready)
+            following = multiply(pix_peer(p + 1))
             for z in far_first:
-                if p or z:
-                    send(source.at[t], target.at[mine], sems, p, z)
+                send(source.at[t], target.at[mine], sems, p, z)
+            return following
+
+        put(me, lax.fori_loop(1, npix, go, multiply(pix_peer(1))))
+        for z in far_first:
+            if z:
+                send(source.at[me], target.at[mine], sems, 0, z)
         target[pl.ds(mine, 1)] = source[pl.ds(me, 1)]
 
     state_row = lax.broadcasted_iota(jnp.int32, (rows, LANES), 0).astype(jnp.float32)
@@ -250,7 +265,8 @@
         for n in range(len(groups)):
             total = column_fold(sums[n * slots : (n + 1) * slots])
             col_recv[i, pl.ds(me, 1), n : n + 1] = total[None]
-        for p in range(1, npix):
+        @pl.loop(1, npix)
+        def send_columns(p):
             send(col_recv.at[i, me], col_recv.at[i, me], col_sem.at[i], p, 0)
 
         new_pixel = jnp.clip(pixel_level - (duals - weights_ref[...]), 0.0, 1.0)

time: 33.8 us -> 34.2 us (1.012)
  Pallas kernels: 32.9 us -> 33.3 us
    pallas_call x1, Pallas kernels: 31.5 us -> 32 us  [local(): pl.pallas_call(functools.partial(kernel, npix, nsite), out_shape=results,...]
where the time goes in v5:
time: 34.2 us; the launch traced here: 34 us
  Pallas kernels  33.3 us (97%)
  between operations  0.64 us (2%)
    pallas_call x1, Pallas kernels, local(): pl.pallas_call(functools.partial(kernel, npix, nsite), out_shape=results,...  32 us
    pallas_call x1, Pallas kernels, local(): pl.pallas_call(hand_on, out_shape=results, in_specs=[hbm] * 3, out_specs=...  1.38 us

profile of v5, /device:TPU:0, one launch (start us, length us, event | category | flops | bytes accessed | tf_op | source)
XLA Modules:
  0.0 34.0 jit_solution(10177600920347100303)
XLA Ops:
  0.6 32.0 %shard_map.112 = (f32[1,128]{1,0:T(1,128)}, f32[32,128]{1,0:T(8,128)}, f32[32,128]{1,0:T(8,128)}) custom-call(s32[16,256,128]{2,1,0:T(8,128)} %margins_hbm.1, s32[1,16]{1,0:T(1,128)} %bitcast.13, s32[1,128]{1,0:T(1,128)} %bitcast.14, f32[16,256]{1,0:T(8,128)} %gain_hbm.1, f32[1,128]{1,0:T(1,128)} %bitcast.15, f32[32,128]{1,0:T(8,128)} %bitcast.10, ...), custom_call_target="tpu_custom_call" | custom-call | tf_op jit(solution)/shard_map/pallas_call | solution.py:358
  32.6 1.4 %shard_map.113 = (f32[1,128]{1,0:T(1,128)}, f32[32,128]{1,0:T(8,128)}, f32[32,128]{1,0:T(8,128)}) custom-call(f32[1,128]{1,0:T(1,128)} %get-tuple-element.9.site_in, f32[32,128]{1,0:T(8,128)} %get-tuple-element.10.pixel_in, f32[32,128]{1,0:T(8,128)} %get-tuple-element.11.dual_in), custom_call_target="tpu_custom_call" | custom-call | tf_op jit(solution)/shard_map/pallas_call | solution.py:405

commit v6 on v4

--- a/solution.py
+++ b/solution.py
@@ -48,6 +48,7 @@
     col_recv,
     push_send,
     push_recv,
+    parts,
     margin_sem,
     small_sem,
     dual_sem,
@@ -63,11 +64,14 @@
     here = lax.axis_index("site")
     mine = here * npix + me
 
+    pix_ids = [me] + [lax.rem(me + step, npix) for step in range(1, npix)]
+    site_ids = [here] + [lax.rem(here + step, nsite) for step in range(1, nsite)]
+
     def pix_peer(step):
-        return lax.rem(me + step, npix)
+        return pix_ids[step]
 
     def site_peer(step):
-        return lax.rem(here + step, nsite)
+        return site_ids[step]
 
     far_first = sorted(range(nsite), key=lambda z: -min(z, nsite - z))
     peers = [(p, z) for p in list(range(1, npix)) + [0] for z in far_first if p or z]
@@ -92,16 +96,16 @@
         part = pl.ds(t * cap, cap)
         return pltpu.make_async_copy(margins_hbm.at[part], margins_v.at[part], margin_sem.at[t])
 
-    for copy in small:
-        copy.start()
-    for t in range(npix):
-        margin_copy(t).start()
-
     barrier = pltpu.get_barrier_semaphore()
     for p, z in peers:
         pl.semaphore_signal(
             barrier, inc=1, device_id=(pix_peer(p), site_peer(z)), device_id_type=MESH
         )
+
+    for copy in small:
+        copy.start()
+    for t in range(npix):
+        margin_copy(t).start()
 
     def send(src, dst, sems, p, z):
         pltpu.make_async_remote_copy(
@@ -191,45 +195,76 @@
 
     lax.fori_loop(0, npix, build, 0)
 
-    def send_products(values, source, target, sems, turn):
+    order = list(range(1, npix)) + [0]
+
+    def multiply(lhs, t):
+        return jnp.dot(lhs, tiles_t[t], preferred_element_type=jnp.float32)
+
+    def put(target, t, products):
+        for h in range(halves):
+            target[t, h * cap : (h + 1) * cap, :] = products[:cap, h * LANES : (h + 1) * LANES]
+
+    def send_lines(source, target, sems, arrival, p):
+        t = pix_peer(p)
+        for z in far_first:
+            if p or z:
+                pltpu.make_async_remote_copy(
+                    src_ref=source.at[t],
+                    dst_ref=target.at[mine],
+                    send_sem=sems.at[0],
+                    recv_sem=arrival,
+                    device_id=(t, site_peer(z)),
+                    device_id_type=MESH,
+                ).start()
+
+    def send_products(values, source, target, sems):
         lhs = spread_sites(values)
-        order = [pix_peer(p) for p in list(range(1, npix)) + [0]]
-
-        def multiply(t):
-            if turn:
-                tiles_t[t] = tiles[t].T
-            return jnp.dot(lhs, tiles_t[t], preferred_element_type=jnp.float32)
-
-        ready = multiply(order[0])
-        for n, t in enumerate(order):
-            products = ready
-            for h in range(halves):
-                source[t, h * cap : (h + 1) * cap, :] = products[
-                    :cap, h * LANES : (h + 1) * LANES
-                ]
+        ready = multiply(lhs, pix_peer(order[0]))
+        for n, p in enumerate(order):
+            put(source, pix_peer(p), ready)
             if n + 1 < npix:
-                ready = multiply(order[n + 1])
-            p = (n + 1) % npix
-            for z in far_first:
-                if p or z:
-                    send(source.at[t], target.at[mine], sems, p, z)
+                ready = multiply(lhs, pix_peer(order[n + 1]))
+            send_lines(source, target, sems, sems.at[1 + here], p)
         target[pl.ds(mine, 1)] = source[pl.ds(me, 1)]
 
+    lhs = spread_sites(jnp.ones((1, LANES), jnp.float32))
+    for t in range(npix):
+        tiles_t[t] = tiles[t].T
+        put(row_send, t, multiply(lhs, t))
+
     state_row = lax.broadcasted_iota(jnp.int32, (rows, LANES), 0).astype(jnp.float32)
 
-    def gather_rows(buffer):
-        def group(z, total):
-            for p in range(npix):
-                s = z * npix + p
-                for c in range(cap):
-                    line = row_recv[s, halves * cap + c : halves * cap + c + 1, :]
-                    offset = state_row - line * halves
-                    for h in range(halves):
-                        line = buffer[s, h * cap + c : h * cap + c + 1, :]
-                        total = total + jnp.where(offset == h, line, 0.0)
-            return total
-
-        return lax.fori_loop(0, nsite, group, jnp.zeros((rows, LANES), jnp.float32))
+    def gather_group(z, buffer):
+        total = jnp.zeros((rows, LANES), jnp.float32)
+        for p in range(npix):
+            s = z * npix + p
+            for c in range(cap):
+                line = row_recv[s, halves * cap + c : halves * cap + c + 1, :]
+                offset = state_row - line * halves
+                for h in range(halves):
+                    line = buffer[s, h * cap + c : h * cap + c + 1, :]
+                    total = total + jnp.where(offset == h, line, 0.0)
+        parts[z] = total
+
+    def gather_rows(buffer, arrivals):
+        def wait_for(z, count):
+            if arrivals is not None:
+                part = buffer.at[pl.ds(z * npix, count)]
+                pltpu.make_async_copy(part, part, arrivals.at[1 + z]).wait()
+
+        wait_for(here, npix - 1)
+        gather_group(here, buffer)
+
+        @pl.loop(1, nsite)
+        def others(step):
+            z = lax.rem(here + step, nsite)
+            wait_for(z, npix)
+            gather_group(z, buffer)
+
+        total = parts[0]
+        for z in range(1, nsite):
+            total = total + parts[z]
+        return total
 
     site_level = site_ref[...]
     pixel_level = pixel_ref[...]
@@ -256,7 +291,9 @@
         new_pixel = jnp.clip(pixel_level - (duals - weights_ref[...]), 0.0, 1.0)
         ahead = 2.0 * new_pixel - pixel_level
         if i == 0:
-            send_products(jnp.ones((1, LANES), jnp.float32), row_send, row_recv, row_sem, True)
+            for p in order:
+                send_lines(row_send, row_recv, row_sem, row_sem.at[1], p)
+            row_recv[pl.ds(mine, 1)] = row_send[pl.ds(me, 1)]
 
         drain(col_recv.at[i], col_sem.at[i, 1])
         pulled = col_recv[i, 0]
@@ -266,13 +303,12 @@
             column_sum = pulled[1:2]
         new_site = jnp.clip(site_level - (price_ref[...] - pulled[0:1] / column_sum), 0.0, 1.0)
         send_products(
-            2.0 * new_site - site_level, push_send.at[i], push_recv.at[i], push_sem.at[i], False
+            2.0 * new_site - site_level, push_send.at[i], push_recv.at[i], push_sem.at[i]
         )
         if i == 0:
             drain(row_recv, row_sem.at[1])
-            row_sum = gather_rows(row_recv) + 1.0
-        drain(push_recv.at[i], push_sem.at[i, 1])
-        pushed = gather_rows(push_recv.at[i])
+            row_sum = gather_rows(row_recv, None) + 1.0
+        pushed = gather_rows(push_recv.at[i], push_sem.at[i])
         duals = jnp.maximum(duals + (ahead - pushed) / row_sum, 0.0)
         if i < ITERS - 1:
             share_duals(i + 1, duals)
@@ -365,12 +401,13 @@
             pltpu.VMEM((ITERS, npix, 2, LANES), f32),
             pltpu.VMEM((ITERS, npix, halves * cap, LANES), f32),
             pltpu.VMEM((ITERS, devices, halves * cap, LANES), f32),
+            pltpu.VMEM((nsite, rows, LANES), f32),
             dma((npix,)),
             dma((8,)),
             dma((ITERS, 2)),
             dma((2,)),
             dma((ITERS, 2)),
-            dma((ITERS, 2)),
+            dma((ITERS, 1 + nsite)),
         ],
         compiler_params=pltpu.CompilerParams(
             collective_id=0, has_side_effects=True, vmem_limit_bytes=60 * 1024 * 1024

time: 33.8 us -> 33.7 us (level)
  no operation moved by 1% of the time
where the time goes in v6:
time: 33.7 us; the launch traced here: 33.4 us
  Pallas kernels  32.8 us (97%)
  between operations  0.64 us (2%)
    pallas_call x1, Pallas kernels, local(): pl.pallas_call(functools.partial(kernel, npix, nsite), out_shape=results,...  31.4 us
    pallas_call x1, Pallas kernels, local(): pl.pallas_call(hand_on, out_shape=results, in_specs=[hbm] * 3, out_specs=...  1.38 us

profile of v6, /device:TPU:0, one launch (start us, length us, event | category | flops | bytes accessed | tf_op | source)
XLA Modules:
  0.0 33.4 jit_solution(18273183408891671689)
XLA Ops:
  0.6 31.4 %shard_map.112 = (f32[1,128]{1,0:T(1,128)}, f32[32,128]{1,0:T(8,128)}, f32[32,128]{1,0:T(8,128)}) custom-call(s32[16,256,128]{2,1,0:T(8,128)} %margins_hbm.1, s32[1,16]{1,0:T(1,128)} %bitcast.13, s32[1,128]{1,0:T(1,128)} %bitcast.14, f32[16,256]{1,0:T(8,128)} %gain_hbm.1, f32[1,128]{1,0:T(1,128)} %bitcast.15, f32[32,128]{1,0:T(8,128)} %bitcast.10, ...), custom_call_target="tpu_custom_call" | custom-call | tf_op jit(solution)/shard_map/pallas_call | solution.py:378
  32.0 1.4 %shard_map.113 = (f32[1,128]{1,0:T(1,128)}, f32[32,128]{1,0:T(8,128)}, f32[32,128]{1,0:T(8,128)}) custom-call(f32[1,128]{1,0:T(1,128)} %get-tuple-element.9.site_in, f32[32,128]{1,0:T(8,128)} %get-tuple-element.10.pixel_in, f32[32,128]{1,0:T(8,128)} %get-tuple-element.11.dual_in), custom_call_target="tpu_custom_call" | custom-call | tf_op jit(solution)/shard_map/pallas_call | solution.py:426

commit v7 on v6

--- a/solution.py
+++ b/solution.py
@@ -49,6 +49,8 @@
     push_send,
     push_recv,
     parts,
+    level_recv,
+    level_sem,
     margin_sem,
     small_sem,
     dual_sem,
@@ -231,35 +233,36 @@
     for t in range(npix):
         tiles_t[t] = tiles[t].T
         put(row_send, t, multiply(lhs, t))
+    for p in range(1, npix):
+        send(row_send.at[pix_peer(p)], row_recv.at[me], row_sem, p, 0)
+    row_recv[pl.ds(me, 1)] = row_send[pl.ds(me, 1)]
 
     state_row = lax.broadcasted_iota(jnp.int32, (rows, LANES), 0).astype(jnp.float32)
 
-    def gather_group(z, buffer):
+    def gather_group(z, buffer, first_line):
         total = jnp.zeros((rows, LANES), jnp.float32)
         for p in range(npix):
-            s = z * npix + p
             for c in range(cap):
-                line = row_recv[s, halves * cap + c : halves * cap + c + 1, :]
-                offset = state_row - line * halves
+                at = rows + p * cap + c
+                offset = state_row - level_recv[z, at : at + 1, :] * halves
                 for h in range(halves):
-                    line = buffer[s, h * cap + c : h * cap + c + 1, :]
+                    line = buffer[first_line + p, h * cap + c : h * cap + c + 1, :]
                     total = total + jnp.where(offset == h, line, 0.0)
-        parts[z] = total
+        return total
 
     def gather_rows(buffer, arrivals):
         def wait_for(z, count):
-            if arrivals is not None:
-                part = buffer.at[pl.ds(z * npix, count)]
-                pltpu.make_async_copy(part, part, arrivals.at[1 + z]).wait()
+            part = buffer.at[pl.ds(z * npix, count)]
+            pltpu.make_async_copy(part, part, arrivals.at[1 + z]).wait()
 
         wait_for(here, npix - 1)
-        gather_group(here, buffer)
+        parts[here] = gather_group(here, buffer, here * npix)
 
         @pl.loop(1, nsite)
         def others(step):
             z = lax.rem(here + step, nsite)
             wait_for(z, npix)
-            gather_group(z, buffer)
+            parts[z] = gather_group(z, buffer, z * npix)
 
         total = parts[0]
         for z in range(1, nsite):
@@ -291,9 +294,14 @@
         new_pixel = jnp.clip(pixel_level - (duals - weights_ref[...]), 0.0, 1.0)
         ahead = 2.0 * new_pixel - pixel_level
         if i == 0:
-            for p in order:
-                send_lines(row_send, row_recv, row_sem, row_sem.at[1], p)
-            row_recv[pl.ds(mine, 1)] = row_send[pl.ds(me, 1)]
+            drain(row_recv, row_sem.at[1])
+            for p in range(npix):
+                at = rows + p * cap
+                level_recv[here, at : at + cap, :] = row_recv[p, halves * cap :, :]
+            level_recv[here, :rows, :] = gather_group(here, row_recv, 0)
+            for z in far_first:
+                if z:
+                    send(level_recv.at[here], level_recv.at[here], level_sem, 0, z)
 
         drain(col_recv.at[i], col_sem.at[i, 1])
         pulled = col_recv[i, 0]
@@ -306,8 +314,11 @@
             2.0 * new_site - site_level, push_send.at[i], push_recv.at[i], push_sem.at[i]
         )
         if i == 0:
-            drain(row_recv, row_sem.at[1])
-            row_sum = gather_rows(row_recv, None) + 1.0
+            drain(level_recv, level_sem.at[1])
+            row_sum = level_recv[0, :rows, :]
+            for z in range(1, nsite):
+                row_sum = row_sum + level_recv[z, :rows, :]
+            row_sum = row_sum + 1.0
         pushed = gather_rows(push_recv.at[i], push_sem.at[i])
         duals = jnp.maximum(duals + (ahead - pushed) / row_sum, 0.0)
         if i < ITERS - 1:
@@ -325,6 +336,7 @@
     )
 
     drain(row_recv, row_sem.at[0])
+    drain(level_recv, level_sem.at[0])
     for i in range(ITERS):
         drain(dual_all.at[i], dual_sem.at[i, 0])
         drain(col_recv.at[i], col_sem.at[i, 0])
@@ -397,11 +409,13 @@
             pltpu.VMEM((npix, cap * sites, width), jnp.bfloat16),
             pltpu.VMEM((ITERS, npix, rows, LANES), jnp.bfloat16),
             pltpu.VMEM((npix, (halves + 1) * cap, LANES), f32),
-            pltpu.VMEM((devices, (halves + 1) * cap, LANES), f32),
+            pltpu.VMEM((npix, (halves + 1) * cap, LANES), f32),
             pltpu.VMEM((ITERS, npix, 2, LANES), f32),
             pltpu.VMEM((ITERS, npix, halves * cap, LANES), f32),
             pltpu.VMEM((ITERS, devices, halves * cap, LANES), f32),
             pltpu.VMEM((nsite, rows, LANES), f32),
+            pltpu.VMEM((nsite, rows + slots, LANES), f32),
+            dma((2,)),
             dma((npix,)),
             dma((8,)),
             dma((ITERS, 2)),

time: 33.7 us -> 33.7 us (level)
  no operation moved by 1% of the time
where the time goes in v7:
time: 33.7 us; the launch traced here: 33.4 us
  Pallas kernels  32.8 us (97%)
  between operations  0.64 us (2%)
    pallas_call x1, Pallas kernels, local(): pl.pallas_call(functools.partial(kernel, npix, nsite), out_shape=results,...  31.4 us
    pallas_call x1, Pallas kernels, local(): pl.pallas_call(hand_on, out_shape=results, in_specs=[hbm] * 3, out_specs=...  1.38 us

profile of v7, /device:TPU:0, one launch (start us, length us, event | category | flops | bytes accessed | tf_op | source)
XLA Modules:
  0.0 33.4 jit_solution(15477216837951780502)
XLA Ops:
  0.6 31.4 %shard_map.112 = (f32[1,128]{1,0:T(1,128)}, f32[32,128]{1,0:T(8,128)}, f32[32,128]{1,0:T(8,128)}) custom-call(s32[16,256,128]{2,1,0:T(8,128)} %margins_hbm.1, s32[1,16]{1,0:T(1,128)} %bitcast.13, s32[1,128]{1,0:T(1,128)} %bitcast.14, f32[16,256]{1,0:T(8,128)} %gain_hbm.1, f32[1,128]{1,0:T(1,128)} %bitcast.15, f32[32,128]{1,0:T(8,128)} %bitcast.10, ...), custom_call_target="tpu_custom_call" | custom-call | tf_op jit(solution)/shard_map/pallas_call | solution.py:390
  32.0 1.4 %shard_map.113 = (f32[1,128]{1,0:T(1,128)}, f32[32,128]{1,0:T(8,128)}, f32[32,128]{1,0:T(8,128)}) custom-call(f32[1,128]{1,0:T(1,128)} %get-tuple-element.9.site_in, f32[32,128]{1,0:T(8,128)} %get-tuple-element.10.pixel_in, f32[32,128]{1,0:T(8,128)} %get-tuple-element.11.dual_in), custom_call_target="tpu_custom_call" | custom-call | tf_op jit(solution)/shard_map/pallas_call | solution.py:440

commit v8 on v7

--- a/solution.py
+++ b/solution.py
@@ -206,9 +206,9 @@
         for h in range(halves):
             target[t, h * cap : (h + 1) * cap, :] = products[:cap, h * LANES : (h + 1) * LANES]
 
-    def send_lines(source, target, sems, arrival, p):
+    def send_lines(source, target, sems, arrival, p, sites):
         t = pix_peer(p)
-        for z in far_first:
+        for z in sites:
             if p or z:
                 pltpu.make_async_remote_copy(
                     src_ref=source.at[t],
@@ -226,7 +226,10 @@
             put(source, pix_peer(p), ready)
             if n + 1 < npix:
                 ready = multiply(lhs, pix_peer(order[n + 1]))
-            send_lines(source, target, sems, sems.at[1 + here], p)
+            send_lines(source, target, sems, sems.at[1 + here], p, far_first[:1])
+        for z in far_first[1:]:
+            for p in order:
+                send_lines(source, target, sems, sems.at[1 + here], p, [z])
         target[pl.ds(mine, 1)] = source[pl.ds(me, 1)]
 
     lhs = spread_sites(jnp.ones((1, LANES), jnp.float32))

time: 33.7 us -> 34.4 us (1.021)
  Pallas kernels: 32.8 us -> 33.5 us
    pallas_call x1, Pallas kernels: 31.4 us -> 32.1 us  [local(): pl.pallas_call(functools.partial(kernel, npix, nsite), out_shape=results,...]
where the time goes in v8:
time: 34.4 us; the launch traced here: 34.1 us
  Pallas kernels  33.5 us (97%)
  between operations  0.64 us (2%)
    pallas_call x1, Pallas kernels, local(): pl.pallas_call(functools.partial(kernel, npix, nsite), out_shape=results,...  32.1 us
    pallas_call x1, Pallas kernels, local(): pl.pallas_call(hand_on, out_shape=results, in_specs=[hbm] * 3, out_specs=...  1.38 us

profile of v8, /device:TPU:0, one launch (start us, length us, event | category | flops | bytes accessed | tf_op | source)
XLA Modules:
  0.0 34.1 jit_solution(1412808947121039391)
XLA Ops:
  0.6 32.1 %shard_map.112 = (f32[1,128]{1,0:T(1,128)}, f32[32,128]{1,0:T(8,128)}, f32[32,128]{1,0:T(8,128)}) custom-call(s32[16,256,128]{2,1,0:T(8,128)} %margins_hbm.1, s32[1,16]{1,0:T(1,128)} %bitcast.13, s32[1,128]{1,0:T(1,128)} %bitcast.14, f32[16,256]{1,0:T(8,128)} %gain_hbm.1, f32[1,128]{1,0:T(1,128)} %bitcast.15, f32[32,128]{1,0:T(8,128)} %bitcast.10, ...), custom_call_target="tpu_custom_call" | custom-call | tf_op jit(solution)/shard_map/pallas_call | solution.py:393
  32.7 1.4 %shard_map.113 = (f32[1,128]{1,0:T(1,128)}, f32[32,128]{1,0:T(8,128)}, f32[32,128]{1,0:T(8,128)}) custom-call(f32[1,128]{1,0:T(1,128)} %get-tuple-element.9.site_in, f32[32,128]{1,0:T(8,128)} %get-tuple-element.10.pixel_in, f32[32,128]{1,0:T(8,128)} %get-tuple-element.11.dual_in), custom_call_target="tpu_custom_call" | custom-call | tf_op jit(solution)/shard_map/pallas_call | solution.py:443
